TPU v7x, 256 devices: a whole 4x4x8 slice. The times are simulated.
256 devices in a mesh: dp: 4 (over y), ctx: 64 (over x, z, core).
Axes of the slice: x: 4, y: 4, z: 8, core: 2. Of those that a mesh axis runs over, the one named last changes fastest.
Arguments:
- mamba_input: bfloat16 [32768, 4096], P(('dp', 'ctx')), parts along dimension 0, may hold values from -6 to 6
- gate_branch: bfloat16 [32768, 4096], P(('dp', 'ctx')), parts along dimension 0, may hold values from -6 to 6
- step_size: bfloat16 [32768, 4096], P(('dp', 'ctx')), parts along dimension 0, may hold values from 0.5 to 24576
- decay_rates: float32 [16384, 16], P('dp'), parts along dimension 0, may hold values from -0.07 to 0
- input_map: bfloat16 [32768, 16], P(('dp', 'ctx')), parts along dimension 0, may hold values from -3 to 3
- output_map: bfloat16 [32768, 16], P(('dp', 'ctx')), parts along dimension 0, may hold values from -3 to 3
- mixing_weight: bfloat16 [4, 4096], replicated, may hold values from -3 to 3
- mixing_bias: bfloat16 [4096], replicated, may hold values from -3 to 3
- skip_gain: float32 [4096], replicated, may hold values from 0.5 to 1.5
- segments: int32 [32768], P('dp'), parts along dimension 0, may hold values from 0 to 3, never falling along the last dimension, each value on 1 to 6144 neighbouring positions
- query_rows: bfloat16 [32768, 2048], P(('dp', 'ctx')), parts along dimension 0, may hold values from -7 to 7
- key_rows: bfloat16 [32768, 512], P(('dp', 'ctx')), parts along dimension 0, may hold values from -4 to 4
- value_rows: bfloat16 [32768, 512], P(('dp', 'ctx')), parts along dimension 0, may hold values from -6 to 6
Outputs:
- mamba_output: bfloat16 [32768, 4096], P(('dp', 'ctx')), parts along dimension 0
- attention_output: bfloat16 [32768, 2048], P(('dp', 'ctx')), parts along dimension 0
There are 4 independent parts, one for each index of `dp`. A program takes and returns all parts, laid end to end along the dimension named above; an argument that names none is the same for every part. Nothing has to cross between parts.
Inputs may be any that keep to these rules, and one draw needn't show every extreme that they name: `segments`: each of the 4 documents is one run of consecutive positions, numbered in order; the longest has exactly 6144 positions.
All inputs are finite; a program needn't handle non-finite values.
Results may differ from a plain program's by a relative error of at most 0.005.
Values may be sent and summed in bfloat16 or wider, within the bound.
A program may use at most 128 MiB of HBM per device.

v0:
```python
import jax
import jax.numpy as jnp
from jax import lax
from jax.sharding import PartitionSpec as P

KW = 4
HQ = 16


def shifted(value, axis, by):
    count = lax.axis_size(axis)
    pairs = [(i, i + by) for i in range(count) if 0 <= i + by < count]
    return lax.ppermute(value, axis, pairs)


def causal_mixing(extended, extended_ids, mixing_weight, mixing_bias):
    local_rows = extended.shape[0] - (KW - 1)
    here_ids = extended_ids[KW - 1 :]
    summed = mixing_bias.astype(jnp.float32)[None, :] + mixing_weight[KW - 1].astype(jnp.float32)[
        None, :
    ] * extended[KW - 1 :].astype(jnp.float32)
    for delay in range(1, KW):
        earlier = extended[KW - 1 - delay : KW - 1 - delay + local_rows].astype(jnp.float32)
        allowed = (extended_ids[KW - 1 - delay : KW - 1 - delay + local_rows] == here_ids).astype(
            jnp.float32
        )[:, None]
        summed = (
            summed + mixing_weight[KW - 1 - delay].astype(jnp.float32)[None, :] * earlier * allowed
        )
    return jax.nn.silu(summed).astype(jnp.bfloat16)


def decay_terms(step_row, decay_rates, fresh):
    exponent = step_row.astype(jnp.float32)[:, None] * decay_rates
    factor = jnp.where(fresh > 0, jnp.float32(0.0), jnp.exp(exponent))
    weight = jnp.where(fresh > 0, jnp.float32(1.0), jnp.sqrt(-jnp.expm1(2.0 * exponent)))
    return (factor, weight)


def attend_block(block_q, block_pos, keys_all, values_all, segments):
    score_scale = block_q.shape[1] ** (-0.5)
    scores = (
        lax.dot_general(
            block_q, keys_all, (((1,), (1,)), ((), ())), preferred_element_type=jnp.float32
        )
        * score_scale
    )
    key_pos = jnp.arange(keys_all.shape[0], dtype=jnp.int32)
    query_ids = jnp.take(segments, block_pos)
    allowed = (key_pos[None, :] <= block_pos[:, None]) & (segments[None, :] == query_ids[:, None])
    masked = jnp.where(allowed, scores, jnp.float32(-1e30))
    row_max = jnp.max(masked, axis=1, keepdims=True)
    exp_terms = jnp.where(allowed, jnp.exp(masked - row_max), jnp.float32(0.0))
    row_total = jnp.sum(exp_terms, axis=1, keepdims=True)
    probs = (exp_terms / row_total).astype(jnp.bfloat16)
    return jnp.dot(probs, values_all, preferred_element_type=jnp.float32).astype(jnp.bfloat16)


def on_device(
    mamba_input,
    gate_branch,
    step_size,
    decay_rates,
    input_map,
    output_map,
    mixing_weight,
    mixing_bias,
    skip_gain,
    segments,
    query_rows,
    key_rows,
    value_rows,
):
    members = lax.axis_size("ctx")
    my_index = lax.axis_index("ctx")
    local_rows = mamba_input.shape[0]
    channels = mamba_input.shape[1]
    states = decay_rates.shape[1]
    last_rows = shifted(mamba_input[local_rows - (KW - 1) :], "ctx", 1)
    extended = jnp.concatenate([last_rows, mamba_input], axis=0)
    padded_ids = jnp.concatenate([jnp.full((KW - 1,), -1, jnp.int32), segments])
    extended_ids = lax.dynamic_slice_in_dim(padded_ids, my_index * local_rows, local_rows + KW - 1)
    conved = causal_mixing(extended, extended_ids, mixing_weight, mixing_bias)
    previous = extended_ids[KW - 2 : KW - 2 + local_rows]
    here_ids = extended_ids[KW - 1 :]
    fresh = ((here_ids != previous) & (previous >= 0)).astype(jnp.int32)
    inputs = (conved, step_size, input_map, output_map, fresh)

    def forward_pass(carry, item):
        carried, product = carry
        drive, step_row, in_row, out_row, fresh_row = item
        factor, weight = decay_terms(step_row, decay_rates, fresh_row)
        carried = factor * carried + weight * (
            in_row.astype(jnp.float32)[None, :] * drive.astype(jnp.float32)[:, None]
        )
        return ((carried, product * factor), None)

    zeros_state = jnp.zeros((channels, states), jnp.float32)
    ones_state = jnp.ones((channels, states), jnp.float32)
    (local_end, product), _ = lax.scan(forward_pass, (zeros_state, ones_state), inputs)

    def link(repeat, incoming):
        return shifted(product * incoming + local_end, "ctx", 1)

    incoming = lax.fori_loop(0, members - 1, link, zeros_state)

    def replay(carried, item):
        drive, step_row, in_row, out_row, fresh_row = item
        factor, weight = decay_terms(step_row, decay_rates, fresh_row)
        carried = factor * carried + weight * (
            in_row.astype(jnp.float32)[None, :] * drive.astype(jnp.float32)[:, None]
        )
        return (carried, jnp.sum(carried * out_row.astype(jnp.float32)[None, :], axis=1))

    _, readout = lax.scan(replay, incoming, inputs)
    mamba_output = (
        (readout + skip_gain[None, :] * conved.astype(jnp.float32))
        * jax.nn.silu(gate_branch.astype(jnp.float32))
    ).astype(jnp.bfloat16)
    head_count = HQ
    query_split = max(1, members // head_count)
    pieces = head_count * query_split
    per_device = pieces // members
    sub_rows = local_rows // query_split
    head_size = query_rows.shape[1] // head_count
    kv_heads = key_rows.shape[1] // head_size
    query_send = (
        query_rows.reshape(query_split, sub_rows, head_count, head_size)
        .transpose(2, 0, 1, 3)
        .reshape(pieces, sub_rows, head_size)
    )
    key_send = jnp.repeat(
        key_rows.reshape(local_rows, kv_heads, head_size).transpose(1, 0, 2),
        members // kv_heads,
        axis=0,
    )
    value_send = jnp.repeat(
        value_rows.reshape(local_rows, kv_heads, head_size).transpose(1, 0, 2),
        members // kv_heads,
        axis=0,
    )
    query_recv, key_recv, value_recv = (
        lax.all_to_all(query_send, "ctx", split_axis=0, concat_axis=1, tiled=True),
        lax.all_to_all(key_send, "ctx", split_axis=0, concat_axis=1, tiled=True),
        lax.all_to_all(value_send, "ctx", split_axis=0, concat_axis=1, tiled=True),
    )
    keys_all = key_recv[0]
    values_all = value_recv[0]
    piece_ids = my_index * per_device + jnp.arange(per_device, dtype=jnp.int32)
    slot_ids = jnp.arange(members * sub_rows, dtype=jnp.int32)
    sources = slot_ids // sub_rows
    inner_rows = slot_ids % sub_rows
    positions = (
        sources[None, :] * local_rows
        + (piece_ids % query_split)[:, None] * sub_rows
        + inner_rows[None, :]
    )
    query_total = per_device * members * sub_rows
    span = min(512, query_total)
    block_queries = query_recv.reshape(query_total // span, span, head_size)
    block_positions = positions.reshape(query_total // span, span)

    def one_block(item):
        return attend_block(item[0], item[1], keys_all, values_all, segments)

    attended = lax.map(one_block, (block_queries, block_positions)).reshape(
        per_device, members * sub_rows, head_size
    )
    returned = lax.all_to_all(attended, "ctx", split_axis=1, concat_axis=0, tiled=True)
    attention_output = (
        returned.reshape(head_count, query_split, sub_rows, head_size)
        .transpose(1, 2, 0, 3)
        .reshape(local_rows, head_count * head_size)
    )
    return (mamba_output, attention_output)


def solution(mesh):
    in_specs = (
        P(("dp", "ctx"), None),
        P(("dp", "ctx"), None),
        P(("dp", "ctx"), None),
        P("dp", None),
        P(("dp", "ctx"), None),
        P(("dp", "ctx"), None),
        P(),
        P(),
        P(),
        P("dp"),
        P(("dp", "ctx"), None),
        P(("dp", "ctx"), None),
        P(("dp", "ctx"), None),
    )
    out_specs = (P(("dp", "ctx"), None), P(("dp", "ctx"), None))
    return jax.shard_map(
        on_device, mesh=mesh, in_specs=in_specs, out_specs=out_specs, check_vma=False
    )
```

profile of v0, /device:TPU:22, one launch (start us, length us, event | category | flops | bytes accessed | tf_op | source)
XLA Modules:
  0.0 1791.1 jit_solution(7112839683867607369)
XLA Ops:
  2.8 12.2 all-to-all-start
  15.1 16.6 all-to-all-done
  44.2 44.6 %collective-permute-done.1 = bf16[3,4096]{1,0:T(4,128)(2,1)S(1)} collective-permute-done((bf16[3,4096]{1,0:T(4,128)(2,1)S(1)}, bf16[3,4096]{1,0:T(4,128)(2,1)S(1)}, u32[]{:S(2)}, u32[]{:S(2)}) %collective-permute-start.1) | collective-permute-done | bytes 24608 | tf_op jit(solution)/shard_map/ppermute | solution.py:13
  92.6 9.2 all-to-all-start.2
  101.8 326.3 %while.48 = (s32[]{:T(128)}, f32[4096,16]{0,1:T(8,128)S(1)}, f32[4096,16]{0,1:T(8,128)S(1)}, s32[128]{0:T(128)S(1)}, bf16[128,4096]{1,0:T(8,128)(2,1)}, /*index=...) while((s32[]{:T(128)}, f32[4096,16]{0,1:T(8,128)S(1)}, ...), condition=%wide.region_1.2_spmd.clone, body=%wide.region_0.1_spmd.clone.sunk | while | flops 794644 | bytes 1392949 | solution.py:100
  429.3 94.0 %while.47 = (s32[]{:T(128)}, bf16[4,512,128]{2,1,0:T(8,128)(2,1)S(1)}, s32[4,512]{1,0:T(4,128)S(1)}, s32[8192]{0:T(1024)S(1)}, bf16[4,512,128]{2,1,0:T(8,128)(2,...) while((s32[]{:T(128)}, bf16[4,512,128]{2,1,0:T(8,128)(2,1)S(1)}, ...), condition=%wide.region_10.11_spmd, body=%wide.region_7.10_spmd.sunk | while | flops 2244023296 | bytes 54934108 | solution.py:166
  523.3 8.1 copy.55
  532.0 11.5 reduce
  544.5 10.3 all-to-all-start.3
  554.9 627.9 %while.45 = (s32[]{:T(128)}, f32[4096,16]{0,1:T(8,128)S(1)}, f32[4096,16]{0,1:T(8,128)S(1)}, f32[4096,16]{0,1:T(8,128)S(1)}, s32[]{:T(128)}) while((s32[]{:T(128)}, f32[4096,16]{0,1:T(8,128)S(1)}, f32[4096,16]{0,1:T(8,128)S(1)}, f32[4096,16]{0,1:T(8,128)S(1)}, s32[]{:T(128)}) %tuple.118), condition=%wide.region_3.4_spmd, body=%wide.region_2.3_spmd.sunk | while | flops 131074 | bytes 2097253 | solution.py:105
  557.2 15.4 collective-permute-done
  574.5 7.9 collective-permute-done
  584.4 7.9 collective-permute-done
  594.2 7.9 collective-permute-done
  604.1 7.9 collective-permute-done
  613.9 7.9 collective-permute-done
  623.8 7.9 collective-permute-done
  633.6 7.9 collective-permute-done
  643.4 7.9 collective-permute-done
  653.3 7.9 collective-permute-done
  663.1 7.9 collective-permute-done
  673.0 7.9 collective-permute-done
  682.8 7.9 collective-permute-done
  692.7 7.9 collective-permute-done
  702.5 7.9 collective-permute-done
  712.3 7.9 collective-permute-done
  722.2 7.9 collective-permute-done
  732.0 7.9 collective-permute-done
  741.9 7.9 collective-permute-done
  751.7 7.9 collective-permute-done
  761.6 7.9 collective-permute-done
  771.4 7.9 collective-permute-done
  781.2 7.9 collective-permute-done
  791.1 7.9 collective-permute-done
  800.9 7.9 collective-permute-done
  810.8 7.9 collective-permute-done
  820.6 7.9 collective-permute-done
  830.5 7.9 collective-permute-done
  840.3 7.9 collective-permute-done
  850.1 7.9 collective-permute-done
  860.0 7.9 collective-permute-done
  869.8 7.9 collective-permute-done
  879.7 7.9 collective-permute-done
  889.5 7.9 collective-permute-done
  899.4 7.9 collective-permute-done
  909.2 7.9 collective-permute-done
  1076.5 7.9 collective-permute-done
  1182.9 602.7 %while.46 = (s32[]{:T(128)}, f32[4096,16]{0,1:T(8,128)S(1)}, f32[128,4096]{1,0:T(8,128)}, s32[128]{0:T(128)S(1)}, bf16[128,4096]{1,0:T(8,128)(2,1)}, /*index=5*/...) while((s32[]{:T(128)}, f32[4096,16]{0,1:T(8,128)S(1)}, ...), condition=%wide.region_6.7_spmd, body=%wide.region_4.6_spmd.sunk | while | flops 725027 | bytes 917975 | solution.py:115
  (1409 shorter events, 1199.1 us)
Async XLA Ops:
  2.8 28.9 %all-to-all-start = ((bf16[64,32,128]{2,1,0:T(8,128)(2,1)}), bf16[64,32,128]{2,1,0:T(8,128)(2,1)S(1)}, u32[]{:S(2)}, u32[]{:S(2)}) async-start(bf16[64,32,128]{2,1,0:T(8,128)(2,1)} %bitcast.18), calls=%async_computation | async-start | bytes 1048576 | tf_op jit(solution)/shard_map/all_to_all | solution.py:143
  33.6 57.1 %all-to-all-start.1 = ((bf16[64,128,128]{2,1,0:T(8,128)(2,1)}), bf16[64,128,128]{2,1,0:T(8,128)(2,1)}, u32[]{:S(2)}, u32[]{:S(2)}) async-start(bf16[64,128,128]{2,1,0:T(8,128)(2,1)} %bitcast.21), calls=%async_computation.1 | async-start | bytes 4194304 | tf_op jit(solution)/shard_map/all_to_all | solution.py:144
  40.9 47.9 %collective-permute-start.1 = (bf16[3,4096]{1,0:T(4,128)(2,1)S(1)}, bf16[3,4096]{1,0:T(4,128)(2,1)S(1)}, u32[]{:S(2)}, u32[]{:S(2)}) collective-permute-start(bf16[3,4096]{1,0:T(4,128)(2,1)S(1)} %slice.42), channel_id=1, source_target_pairs={{0,1},{1,2},{2,3},{3,4},{4,5},{5,6},{6,7},{7,8},{8,9},{9,10},{10,1... | collective-permute-start | bytes 73736 | tf_op jit(solution)/shard_map/ppermute | solution.py:13
  92.6 335.6 %all-to-all-start.2 = ((bf16[64,128,128]{2,1,0:T(8,128)(2,1)}), bf16[64,128,128]{2,1,0:T(8,128)(2,1)}, u32[]{:S(2)}, u32[]{:S(2)}) async-start(bf16[64,128,128]{2,1,0:T(8,128)(2,1)} %bitcast.24), calls=%async_computation.2 | async-start | bytes 4194304 | tf_op jit(solution)/shard_map/all_to_all | solution.py:145
  544.5 1244.8 %all-to-all-start.3 = ((bf16[64,2,2048]{2,1,0:T(2,128)(2,1)}), bf16[64,2,2048]{2,1,0:T(2,128)(2,1)S(1)}, u32[]{:S(2)}, u32[]{:S(2)}) async-start(bf16[64,2,2048]{2,1,0:T(2,128)(2,1)} %reshape.184), calls=%async_computation.3 | async-start | bytes 1048576 | tf_op jit(solution)/shard_map/all_to_all | solution.py:169
  555.0 17.6 collective-permute-start
  572.6 9.8 collective-permute-start
  582.4 9.8 collective-permute-start
  592.3 9.8 collective-permute-start
  602.1 9.8 collective-permute-start
  612.0 9.8 collective-permute-start
  621.8 9.8 collective-permute-start
  631.7 9.8 collective-permute-start
  641.5 9.8 collective-permute-start
  651.3 9.8 collective-permute-start
  661.2 9.8 collective-permute-start
  671.0 9.8 collective-permute-start
  680.9 9.8 collective-permute-start
  690.7 9.8 collective-permute-start
  700.6 9.8 collective-permute-start
  710.4 9.8 collective-permute-start
  720.3 9.8 collective-permute-start
  730.1 9.8 collective-permute-start
  739.9 9.8 collective-permute-start
  749.8 9.8 collective-permute-start
  759.6 9.8 collective-permute-start
  769.5 9.8 collective-permute-start
  779.3 9.8 collective-permute-start
  789.2 9.8 collective-permute-start
  799.0 9.8 collective-permute-start
  808.8 9.8 collective-permute-start
  818.7 9.8 collective-permute-start
  828.5 9.8 collective-permute-start
  838.4 9.8 collective-permute-start
  848.2 9.8 collective-permute-start
  858.1 9.8 collective-permute-start
  867.9 9.8 collective-permute-start
  877.7 9.8 collective-permute-start
  887.6 9.8 collective-permute-start
  956.5 9.8 collective-permute-start
  966.3 9.8 collective-permute-start
  976.2 9.8 collective-permute-start
  1054.9 9.8 collective-permute-start
  1064.8 9.8 collective-permute-start
  1074.6 9.8 collective-permute-start
  1143.5 9.8 collective-permute-start
  1153.4 9.8 collective-permute-start
  1163.2 9.8 collective-permute-start
  (41 other events, 2825.9 us)
where the time goes:
time: 1810 us; the launch traced here: 1790 us
  waiting for transfers between devices  564 us (31%)
  other arithmetic  428 us (24%)
  local copies, waits for them, and re-layouts  399 us (22%)
  loops' own time  180 us (10%)
  starting transfers between devices  162 us (9%)
  matrix products  56.2 us (3%)
    ppermute x64, waiting for transfers between devices, shifted(): return lax.ppermute(value, axis, pairs)  548 us
    dynamic_update_slice x128, local copies, waits for them, and re-layouts, on_device(): _, readout = lax.scan(replay, incoming, inputs)  207 us
    dynamic_slice x256, local copies, waits for them, and re-layouts, on_device(): lax.scan(forward_pass, (zeros_state, ones_state), inputs)  160 us
    ppermute x64, starting transfers between devices, shifted(): return lax.ppermute(value, axis, pairs)  123 us
    convert_element_type x128, other arithmetic, forward_pass(): drive.astype(jnp.float32)[:, None]  112 us
    convert_element_type x128, other arithmetic, replay(): drive.astype(jnp.float32)[:, None]  111 us
    another operation x1, loops' own time, on_device(): lax.scan(forward_pass, (zeros_state, ones_state), inputs)  93.4 us
    mul x128, other arithmetic, replay(): in_row.astype(jnp.float32)[None, :] * drive.astype(jnp.float32)[:, None]  88.4 us
  transfers between devices with their start and end apart: 68, of which 65 were waited for; matrix products, arithmetic and copies ran while one was open for 42% of the time, Pallas kernels for 0%

commit v1 on v0

v1 whole, which is shorter than its diff:
```python
import functools

import jax
import jax.numpy as jnp
from jax import lax
from jax.experimental import pallas as pl
from jax.experimental.pallas import tpu as pltpu
from jax.sharding import PartitionSpec as P

F32 = jnp.float32
BF16 = jnp.bfloat16
MESH = pl.DeviceIdType.MESH
LOG2E = 1.4426950408889634
LN2 = 0.6931471805599453

ROWS = 128
CH = 4096
NS = 16
PLANES = 4
RING = 16
ZN = 8
HD = 128
GROUP = 4
STEPS = 16
HUGE = 3e38
MASKED = -1e30
OWN = CH // RING
SCALE = LOG2E / HD**0.5
ROW_CONTRACT = (((0,), (0,)), ((), ()))
LANE_CONTRACT = (((1,), (1,)), ((), ()))


def iota(shape, dim):
    return lax.broadcasted_iota(jnp.int32, shape, dim)


def silu(v):
    return v / (1.0 + jnp.exp(-v))


def kernel(
    x_hbm, gate_hbm, step_hbm, decay_ref, in_ref, out_map_ref, taps_ref, bias_ref, skip_ref, seg_ref,
    q_hbm, k_hbm, v_hbm,
    mixed_hbm, attended_hbm,
    xv, gv, sv, halo, u_ref, s_ref, cum_ref, gs_ref, y_ref, ends_ref, rates_ref, rates_t, bb_ref, cc_ref,
    masks_ref, kv, q_in, q_aug, o_buf, m_out, totals, plane_in, plane_total, across_in, spread, entering,
    own_prefix,
    load_sem, halo_sem, qkv_send, qkv_recv, fwd_send, fwd_recv, bwd_send, bwd_recv, sib_send, sib_recv,
    tot_send, tot_recv, acr_send, acr_recv, spr_send, spr_recv, o_send, o_recv, own_sem, store_sem,
):
    dp = lax.axis_index("dp")
    me = lax.axis_index("ctx")
    plane = me // RING
    r = me % RING
    z = r // 2
    core = r % 2

    def at(p, rr):
        return (dp, p * RING + rr)

    def remote(src, dst, send, recv, target):
        return pltpu.make_async_remote_copy(
            src_ref=src, dst_ref=dst, send_sem=send, recv_sem=recv, device_id=target, device_id_type=MESH
        )

    loads = [
        pltpu.make_async_copy(x_hbm, xv, load_sem.at[0]),
        pltpu.make_async_copy(step_hbm, sv, load_sem.at[1]),
        pltpu.make_async_copy(gate_hbm, gv, load_sem.at[2]),
    ]
    for load in loads:
        load.start()

    barrier = pltpu.get_barrier_semaphore()

    @pl.loop(1, RING)
    def _(j):
        pl.semaphore_signal(barrier, inc=1, device_id=at(plane, (r + j) % RING), device_id_type=MESH)

    @pl.loop(1, PLANES)
    def _(j):
        pl.semaphore_signal(barrier, inc=1, device_id=at((plane + j) % PLANES, r), device_id_type=MESH)

    count = PLANES * RING
    pl.semaphore_signal(barrier, inc=1, device_id=(dp, (me + 1) % count), device_id_type=MESH)
    pl.semaphore_signal(barrier, inc=1, device_id=(dp, (me + count - 1) % count), device_id_type=MESH)
    pl.semaphore_wait(barrier, RING - 1 + PLANES - 1 + 2)

    halo_copy = remote(
        x_hbm.at[pl.ds(ROWS - 16, 16), :], halo, halo_sem.at[0], halo_sem.at[1], (dp, (me + 1) % count)
    )
    halo_copy.start()

    def qkv_parts(p):
        return [
            (k_hbm.at[:, pl.ds(pl.multiple_of(p * HD, HD), HD)], kv.at[plane, r, :, pl.ds(HD, HD)]),
            (v_hbm.at[:, pl.ds(pl.multiple_of(p * HD, HD), HD)], kv.at[plane, r, :, pl.ds(2 * HD, HD)]),
            (q_hbm.at[:, pl.ds(pl.multiple_of(p * GROUP * HD, HD), GROUP * HD)], q_in.at[plane]),
        ]

    def qkv_copies(o, parts=(0, 1, 2)):
        p = (plane + o) % PLANES
        pairs = qkv_parts(p)
        return [
            remote(pairs[i][0], pairs[i][1], qkv_send.at[o, i], qkv_recv.at[o, i], at(p, r)) for i in parts
        ]

    for parts in ((0, 1), (2,)):
        for o in range(1, PLANES):
            for copy in qkv_copies(o, parts):
                copy.start()
    own_qkv = [pltpu.make_async_copy(s, d, own_sem.at[i]) for i, (s, d) in enumerate(qkv_parts(plane))]
    for copy in own_qkv:
        copy.start()

    p_ids, t_ids = iota((ROWS, ROWS), 0), iota((ROWS, ROWS), 1)
    perm = (t_ids == (p_ids % 8) * STEPS + p_ids // 8).astype(F32)
    perm_b = perm.astype(BF16)
    ones = jnp.ones((ROWS, ROWS), BF16)

    seg = seg_ref[...].astype(F32)
    block_ids = iota((PLANES * RING, ROWS), 0)

    def seg_row(b):
        return jnp.sum(jnp.where(block_ids == b, seg, 0.0), axis=0, keepdims=True)

    here = jnp.broadcast_to(seg_row(me), (8, ROWS))
    before = jnp.broadcast_to(jnp.where(me > 0, seg_row(me - 1), -1.0), (8, ROWS))
    lane8 = iota((8, ROWS), 1)
    for d in range(1, 4):
        ids = jnp.where(lane8 >= d, pltpu.roll(here, d, 1), pltpu.roll(before, d, 1))
        same = (ids == here).astype(F32)
        masks_ref[d] = jnp.dot((perm * same[0:1]).astype(BF16), ones, preferred_element_type=F32)
        if d == 1:
            fresh = ((ids != here) & (ids >= 0.0)).astype(F32)
            masks_ref[0] = jnp.dot((perm * fresh[0:1]).astype(BF16), ones, preferred_element_type=F32)

    repeat = (iota((NS, NS * 128), 0) == iota((NS, NS * 128), 1) // 128).astype(BF16)
    for src, dst in ((in_ref, bb_ref), (out_map_ref, cc_ref)):
        ordered = jnp.dot(perm_b, src[...], preferred_element_type=F32).astype(BF16)
        dst[...] = jnp.dot(ordered, repeat, preferred_element_type=F32)

    @pl.loop(0, CH // 128)
    def _(cb):
        lanes = pl.ds(pl.multiple_of(cb * 128, 128), 128)
        rates = (jnp.minimum(decay_ref[lanes, :], -1e-30) * LOG2E).T
        rates_t[:, lanes] = rates
        for n in range(NS):
            rates_ref[n, :, lanes] = jnp.broadcast_to(rates[n : n + 1], (8, 128))

    unit = (iota((16, HD), 0) == iota((16, HD), 1)).astype(BF16)
    doc_ids = iota((16, ROWS), 0).astype(F32)

    @pl.loop(0, PLANES * RING // 8)
    def _(g):
        rows = seg_ref[pl.ds(pl.multiple_of(g * 8, 8), 8), :].astype(F32)
        for i in range(8):
            hot = (doc_ids == rows[i : i + 1]).astype(BF16)
            cols = lax.dot_general(hot, unit, ROW_CONTRACT, preferred_element_type=F32)
            kv[g // 2, (g % 2) * 8 + i, :, pl.ds(0, HD)] = cols.astype(BF16)

    for p in range(PLANES):
        ids = seg_row(p * RING + r)
        cold = jnp.where((doc_ids != ids) & (doc_ids < 4.0), MASKED, 0.0).astype(BF16)
        cols = lax.dot_general(cold, unit, ROW_CONTRACT, preferred_element_type=F32).astype(BF16)
        for h in range(GROUP):
            q_aug[p, pl.ds(h * ROWS, ROWS), pl.ds(0, HD)] = cols

    for load in loads:
        load.wait()
    halo_copy.wait()

    W = 256

    @pl.loop(0, CH // W)
    def _(b):
        lanes = pl.ds(pl.multiple_of(b * W, W), W)
        xp = jnp.dot(perm_b, xv[:, lanes], preferred_element_type=F32)
        sp = jnp.dot(perm_b, sv[:, lanes], preferred_element_type=F32)
        gp = jnp.dot(perm_b, gv[:, lanes], preferred_element_type=F32)
        edge = halo[:, lanes].astype(F32)
        first = iota((8, W), 0) == 0
        lead = []
        for d in (3, 2, 1):
            rolled = pltpu.roll(xp[(STEPS - d) * 8 : (STEPS - d + 1) * 8], 1, 0)
            lead.append(jnp.where(first, edge[16 - d : 17 - d], rolled))
        extended = jnp.concatenate(lead + [xp], axis=0)
        taps = taps_ref[:, lanes].astype(F32)
        summed = bias_ref[:, lanes].astype(F32) + taps[3:4] * xp
        for d in range(1, 4):
            allowed = jnp.concatenate([masks_ref[d]] * (W // 128), axis=1)
            earlier = extended[(3 - d) * 8 : (3 - d) * 8 + ROWS]
            summed = summed + taps[3 - d : 4 - d] * earlier * allowed
        u_ref[:, lanes] = silu(summed).astype(BF16).astype(F32)
        fresh = jnp.concatenate([masks_ref[0]] * (W // 128), axis=1)
        steps = jnp.where(fresh > 0.0, HUGE, sp)
        s_ref[:, lanes] = steps
        running = steps[0:8]
        cum_ref[pl.ds(0, 8), lanes] = running
        for i in range(1, STEPS):
            running = running + steps[i * 8 : i * 8 + 8]
            cum_ref[pl.ds(i * 8, 8), lanes] = running
        gs_ref[:, lanes] = silu(gp)

    def chunk(rr, lo=0, n=PLANES):
        return kv.at[pl.ds(lo, n), rr, :, pl.ds(HD, 2 * HD)]

    def fwd(s):
        ref = chunk(2 * ((z + ZN - s + 1) % ZN) + core, 0, 4 if s < 4 else 2)
        return remote(ref, ref, fwd_send.at[s], fwd_recv.at[s], at(plane, 2 * ((z + 1) % ZN) + core))

    def bwd(s):
        ref = chunk(2 * ((z + s - 1) % ZN) + core, 0 if s < 4 else 2, 4 if s < 4 else 2)
        return remote(ref, ref, bwd_send.at[s], bwd_recv.at[s], at(plane, 2 * ((z + ZN - 1) % ZN) + core))

    def sibling(s):
        ref = chunk(2 * ((z + ZN - s) % ZN) + core)
        return remote(ref, ref, sib_send.at[s], sib_recv.at[s], at(plane, 2 * z + 1 - core))

    def ring_first():
        for copy in own_qkv[:2]:
            copy.wait()
        for o in range(1, PLANES):
            for copy in qkv_copies(o, (0, 1)):
                copy.wait_recv()
        fwd(1).start()
        bwd(1).start()
        sibling(0).start()

    def ring_next(s):
        fwd(s).wait_recv()
        bwd(s).wait_recv()
        if s < 4:
            fwd(s + 1).start()
            bwd(s + 1).start()
            sibling(s).start()
            sibling(ZN - s).start()
        else:
            sibling(4).start()

    ring_first()

    sub = iota((8, 128), 0)

    def prefix_parts(lanes):
        total = cum_ref[pl.ds((STEPS - 1) * 8, 8), lanes]
        two = total + pltpu.roll(total, 1, 0)
        four = two + pltpu.roll(two, 2, 0)
        return total, two, four

    @pl.loop(0, CH // 128)
    def _(cb):
        for s in range(1, 4):
            @pl.when(cb == 8 * s)
            def _():
                ring_next(s)

        lanes = pl.ds(pl.multiple_of(cb * 128, 128), 128)
        total, two, four = prefix_parts(lanes)
        spans = [
            (1, jnp.where(sub >= 1, total, HUGE)),
            (2, jnp.where(sub >= 2, two, HUGE)),
            (4, jnp.where(sub >= 4, four, HUGE)),
        ]
        ys = [jnp.zeros((8, 128), F32) for _ in range(STEPS)]
        for n in range(NS):
            rate = rates_ref[n, :, lanes]
            state = jnp.zeros((8, 128), F32)
            for i in range(STEPS):
                rows = pl.ds(i * 8, 8)
                exponent = s_ref[rows, lanes] * rate
                factor = jnp.exp2(exponent)
                square = jnp.tanh(exponent * (-LN2)) * (1.0 + factor * factor)
                weight = square * lax.rsqrt(square)
                drive = u_ref[rows, lanes] * bb_ref[rows, pl.ds(n * 128, 128)]
                state = factor * state + weight * drive
                ys[i] = ys[i] + cc_ref[rows, pl.ds(n * 128, 128)] * state
            for by, span in spans:
                state = state + jnp.exp2(rate * span) * pltpu.roll(state, by, 0)
            totals[pl.ds(n, 1), lanes] = state[7:8]
            ends_ref[n, :, lanes] = jnp.where(sub >= 1, pltpu.roll(state, 1, 0), 0.0)
        for i in range(STEPS):
            y_ref[pl.ds(i * 8, 8), lanes] = ys[i]
        summed = total
        for by in (1, 2, 4):
            summed = summed + jnp.where(sub >= by, pltpu.roll(summed, by, 0), 0.0)
        totals[pl.ds(NS, 8), lanes] = jnp.broadcast_to(summed[7:8], (8, 128))

    def own_lanes(rr):
        return pl.ds(pl.multiple_of(rr * OWN, OWN), OWN)

    def totals_copy(j):
        rr = (r + j) % RING
        return remote(totals.at[:, own_lanes(rr)], plane_in.at[r], tot_send.at[j], tot_recv.at[j], at(plane, rr))

    @pl.loop(1, RING)
    def _(j):
        totals_copy(j).start()

    plane_in[r] = totals[:, own_lanes(r)]
    ring_next(4)

    for copy in own_qkv[2:]:
        copy.wait()
    for o in range(1, PLANES):
        for copy in qkv_copies(o, (2,)):
            copy.wait_recv()
    for p in range(PLANES):
        for h in range(GROUP):
            q_aug[p, pl.ds(h * ROWS, ROWS), pl.ds(HD, HD)] = q_in[p, :, pl.ds(h * HD, HD)]
    for s in range(ZN):
        sibling(s).wait_recv()

    CK = RING * ROWS

    def out_copy(p):
        return remote(
            o_buf.at[p],
            attended_hbm.at[:, pl.ds(pl.multiple_of(plane * GROUP * HD, HD), GROUP * HD)],
            o_send.at[p],
            o_recv.at[plane],
            at(p, r),
        )

    def own_out_copy(p):
        return pltpu.make_async_copy(
            o_buf.at[p],
            attended_hbm.at[:, pl.ds(pl.multiple_of(plane * GROUP * HD, HD), GROUP * HD)],
            own_sem.at[3],
        )

    def attend(p):
        def part(c, carry, last):
            top, acc, total = carry
            keys = kv[c, :, :, pl.ds(0, 2 * HD)].reshape(CK, 2 * HD)
            values = kv[c, :, :, pl.ds(2 * HD, HD)].reshape(CK, HD)
            scores = lax.dot_general(keys, q_aug[p], LANE_CONTRACT, preferred_element_type=F32)
            if last:
                limit = iota((CK, GROUP * ROWS), 1) % ROWS + r * ROWS
                scores = jnp.where(iota((CK, GROUP * ROWS), 0) <= limit, scores, MASKED)
            new_top = jnp.maximum(top, jnp.max(scores, axis=0, keepdims=True) * SCALE)
            probs = jnp.exp2(scores * SCALE - new_top)
            shrink = jnp.exp2(top - new_top)
            total = total * shrink + jnp.sum(probs, axis=0, keepdims=True)
            acc = acc * shrink + lax.dot_general(
                values, probs.astype(BF16), ROW_CONTRACT, preferred_element_type=F32
            )
            return new_top, acc, total

        carry = (
            jnp.full((1, GROUP * ROWS), MASKED, F32),
            jnp.zeros((HD, GROUP * ROWS), F32),
            jnp.zeros((1, GROUP * ROWS), F32),
        )
        carry = lax.fori_loop(0, p, lambda c, held: part(c, held, False), carry)
        _, acc, total = part(p, carry, True)
        result = acc / total
        for h in range(GROUP):
            o_buf[p, :, pl.ds(h * HD, HD)] = result[:, h * ROWS : (h + 1) * ROWS].T.astype(BF16)

        @pl.when(plane != p)
        def _():
            out_copy(p).start()

        @pl.when(plane == p)
        def _():
            own_out_copy(p).start()

    attend(3)

    @pl.loop(1, RING)
    def _(j):
        totals_copy(j).wait_recv()

    own_rates = rates_t[:, own_lanes(r)]
    state = jnp.zeros((NS, OWN), F32)
    length = jnp.zeros((1, OWN), F32)
    for i in range(RING):
        own_prefix[i, pl.ds(0, NS), :] = state
        own_prefix[i, pl.ds(NS, 8), :] = jnp.broadcast_to(length, (8, OWN))
        step = plane_in[i, pl.ds(NS, 1), :]
        state = jnp.exp2(own_rates * step) * state + plane_in[i, pl.ds(0, NS), :]
        length = length + step
    plane_total[pl.ds(0, NS), :] = state
    plane_total[pl.ds(NS, 8), :] = jnp.broadcast_to(length, (8, OWN))

    def across_copy(o):
        p = (plane + o) % PLANES
        return remote(plane_total, across_in.at[plane], acr_send.at[o], acr_recv.at[o], at(p, r))

    for o in range(1, PLANES):
        across_copy(o).start()
    across_in[plane] = plane_total[...]

    attend(1)

    for o in range(1, PLANES):
        across_copy(o).wait_recv()
    state = jnp.zeros((NS, OWN), F32)
    for p in range(PLANES - 1):
        moved = jnp.exp2(own_rates * across_in[p, pl.ds(NS, 1), :]) * state + across_in[p, pl.ds(0, NS), :]
        state = jnp.where(p < plane, moved, state)
    for i in range(RING):
        spread[i] = own_prefix[i, pl.ds(0, NS), :] + jnp.exp2(own_rates * own_prefix[i, pl.ds(NS, 1), :]) * state

    def spread_copy(j):
        rr = (r + j) % RING
        return remote(spread.at[rr], entering.at[:, own_lanes(r)], spr_send.at[j], spr_recv.at[j], at(plane, rr))

    @pl.loop(1, RING)
    def _(j):
        spread_copy(j).start()

    entering[:, own_lanes(r)] = spread[r]

    attend(2)
    attend(0)

    @pl.loop(1, RING)
    def _(j):
        spread_copy(j).wait_recv()

    @pl.loop(0, CH // 128)
    def _(cb):
        lanes = pl.ds(pl.multiple_of(cb * 128, 128), 128)
        total, _, _ = prefix_parts(lanes)
        summed = total
        for by in (1, 2, 4):
            summed = summed + jnp.where(sub >= by, pltpu.roll(summed, by, 0), 0.0)
        lead = jnp.where(sub >= 1, pltpu.roll(summed, 1, 0), 0.0)
        ys = [y_ref[pl.ds(i * 8, 8), lanes] for i in range(STEPS)]
        for n in range(NS):
            rate = rates_ref[n, :, lanes]
            state = jnp.exp2(rate * lead) * entering[pl.ds(n, 1), lanes] + ends_ref[n, :, lanes]
            for i in range(STEPS):
                rows = pl.ds(i * 8, 8)
                left = jnp.exp2(cum_ref[rows, lanes] * rate) * state
                ys[i] = ys[i] + cc_ref[rows, pl.ds(n * 128, 128)] * left
        skip = skip_ref[:, lanes]
        for i in range(STEPS):
            rows = pl.ds(i * 8, 8)
            y_ref[rows, lanes] = (ys[i] + skip * u_ref[rows, lanes]) * gs_ref[rows, lanes]

    @pl.loop(0, CH // 512)
    def _(b):
        lanes = pl.ds(pl.multiple_of(b * 512, 512), 512)
        back = lax.dot_general(perm_b, y_ref[:, lanes].astype(BF16), ROW_CONTRACT, preferred_element_type=F32)
        m_out[:, lanes] = back.astype(BF16)

    store = pltpu.make_async_copy(m_out, mixed_hbm, store_sem)
    store.start()

    for o in range(1, PLANES):
        for copy in qkv_copies(o):
            copy.wait_send()
        across_copy(o).wait_send()
    for s in range(1, 5):
        fwd(s).wait_send()
        bwd(s).wait_send()
    for s in range(ZN):
        sibling(s).wait_send()

    @pl.loop(1, RING)
    def _(j):
        totals_copy(j).wait_send()
        spread_copy(j).wait_send()

    for p in range(PLANES):
        @pl.when(plane != p)
        def _():
            out_copy(p).wait_send()
            pltpu.make_async_remote_copy(
                src_ref=o_buf.at[p],
                dst_ref=attended_hbm.at[:, pl.ds(p * GROUP * HD, GROUP * HD)],
                send_sem=o_send.at[p],
                recv_sem=o_recv.at[p],
                device_id=at(p, r),
                device_id_type=MESH,
            ).wait_recv()

        @pl.when(plane == p)
        def _():
            own_out_copy(p).wait()

    store.wait()


def on_device(
    mamba_input, gate_branch, step_size, decay_rates, input_map, output_map, mixing_weight, mixing_bias,
    skip_gain, segments, query_rows, key_rows, value_rows,
):
    hbm = pl.BlockSpec(memory_space=pl.ANY)
    vmem = pl.BlockSpec(memory_space=pltpu.VMEM)
    big = pltpu.VMEM((ROWS, CH), F32)
    dma = pltpu.SemaphoreType.DMA
    return pl.pallas_call(
        kernel,
        out_shape=(
            jax.ShapeDtypeStruct((ROWS, CH), BF16),
            jax.ShapeDtypeStruct((ROWS, PLANES * GROUP * HD), BF16),
        ),
        in_specs=[hbm] * 3 + [vmem] * 7 + [hbm] * 3,
        out_specs=(hbm, hbm),
        scratch_shapes=[
            pltpu.VMEM((ROWS, CH), BF16),
            pltpu.VMEM((ROWS, CH), BF16),
            pltpu.VMEM((ROWS, CH), BF16),
            pltpu.VMEM((16, CH), BF16),
            big, big, big, big, big,
            pltpu.VMEM((NS, 8, CH), F32),
            pltpu.VMEM((NS, 8, CH), F32),
            pltpu.VMEM((NS, CH), F32),
            pltpu.VMEM((ROWS, NS * 128), F32),
            pltpu.VMEM((ROWS, NS * 128), F32),
            pltpu.VMEM((4, ROWS, ROWS), F32),
            pltpu.VMEM((PLANES, RING, ROWS, 3 * HD), BF16),
            pltpu.VMEM((PLANES, ROWS, GROUP * HD), BF16),
            pltpu.VMEM((PLANES, GROUP * ROWS, 2 * HD), BF16),
            pltpu.VMEM((PLANES, ROWS, GROUP * HD), BF16),
            pltpu.VMEM((ROWS, CH), BF16),
            pltpu.VMEM((NS + 8, CH), F32),
            pltpu.VMEM((RING, NS + 8, OWN), F32),
            pltpu.VMEM((NS + 8, OWN), F32),
            pltpu.VMEM((PLANES, NS + 8, OWN), F32),
            pltpu.VMEM((RING, NS, OWN), F32),
            pltpu.VMEM((NS, CH), F32),
            pltpu.VMEM((RING, NS + 8, OWN), F32),
            dma((3,)), dma((2,)), dma((4, 3)), dma((4, 3)),
            dma((5,)), dma((5,)), dma((5,)), dma((5,)), dma((ZN,)), dma((ZN,)),
            dma((RING,)), dma((RING,)), dma((PLANES,)), dma((PLANES,)), dma((RING,)), dma((RING,)),
            dma((PLANES,)), dma((PLANES,)), dma((4,)), dma(()),
        ],
        compiler_params=pltpu.CompilerParams(
            collective_id=0, has_side_effects=True, vmem_limit_bytes=60 * 2**20
        ),
        name="mixer",
    )(
        mamba_input, gate_branch, step_size, decay_rates, input_map, output_map, mixing_weight,
        mixing_bias.reshape(1, CH), skip_gain.reshape(1, CH), segments.reshape(PLANES * RING, ROWS),
        query_rows, key_rows, value_rows,
    )


def solution(mesh):
    split = P(("dp", "ctx"), None)
    in_specs = (
        split, split, split, P("dp", None), split, split, P(), P(), P(), P("dp"), split, split, split,
    )
    return jax.shard_map(
        on_device, mesh=mesh, in_specs=in_specs, out_specs=(split, split), check_vma=False
    )
```

time: 1810 us -> 95.9 us (0.05)
  the two profiles are of different devices: /device:TPU:22 before, /device:TPU:1 now
where the time goes in v1:
time: 95.9 us; the launch traced here: 95.7 us
  Pallas kernels  84.9 us (89%)
  local copies, waits for them, and re-layouts  10.2 us (11%)
    pallas_call x1, Pallas kernels, on_device(): pl.pallas_call(kernel, out_shape=(jax.ShapeDtypeStruct((ROWS, CH), BF16),...  84.9 us
    unnamed x7, local copies, waits for them, and re-layouts  8.85 us

profile of v1, /device:TPU:1, one launch (start us, length us, event | category | flops | bytes accessed | tf_op | source)
XLA Modules:
  0.0 95.7 jit_solution(17039389156476300079)
XLA Ops:
  0.6 1.3 %reshape.13.bias_ref = bf16[1,4096]{1,0:T(2,128)(2,1)} reshape(bf16[4096]{0:T(1024)(128)(2,1)} %param.20) | data formatting | bytes 16384 | tf_op jit(solution)/shard_map/reshape | solution.py:539
  1.9 1.4 %copy.16.in_ref = bf16[128,16]{1,0:T(8,128)(2,1)} copy(bf16[128,16]{0,1:T(8,128)(2,1)} %param.17) | data formatting | bytes 8192 | tf_op args[4]
  3.3 1.4 %copy.17.out_map_ref = bf16[128,16]{1,0:T(8,128)(2,1)} copy(bf16[128,16]{0,1:T(8,128)(2,1)} %param.18) | data formatting | bytes 8192 | tf_op args[5]
  4.7 2.9 %copy.15.decay_ref = f32[4096,16]{1,0:T(8,128)} copy(f32[4096,16]{0,1:T(8,128)} %param.16) | data formatting | bytes 524288 | tf_op args[3]
  7.6 84.9 %mixer.1 = (bf16[128,4096]{1,0:T(8,128)(2,1)}, bf16[128,2048]{1,0:T(8,128)(2,1)}) custom-call(bf16[128,4096]{1,0:T(8,128)(2,1)} %x_hbm.1, bf16[128,4096]{1,0:T(8,128)(2,1)} %gate_hbm.1, bf16[128,4096]{1,0:T(8,128)(2,1)} %step_hbm.1, f32[4096,16]{1,0:T(8,128)} %copy.15.decay_ref, bf16[128,16]{1,0:T(8,128)(2,1)} %copy.16.in_ref, ...), custom_call_target="tpu_custom_call" | custom-call | tf_op jit(solution)/shard_map/mixer/pallas_call | solution.py:496
  92.5 0.0 copy-start
  92.5 2.3 %copy.20 = bf16[128,4096]{1,0:T(8,128)(2,1)} copy(bf16[128,4096]{1,0:T(8,128)(2,1)} %get-tuple-element.4) | data formatting | bytes 2097152
  94.9 0.0 copy-done
  94.9 0.8 copy.21
Async XLA Ops:
  92.5 2.4 %copy-start = (bf16[128,2048]{1,0:T(8,128)(2,1)S(1)}, bf16[128,2048]{1,0:T(8,128)(2,1)}, u32[]{:S(2)}) copy-start(bf16[128,2048]{1,0:T(8,128)(2,1)} %get-tuple-element.5) | copy-start | bytes 1572868

commit v2 on v1

v2 whole, which is shorter than its diff:
```python
import functools

import jax
import jax.numpy as jnp
from jax import lax
from jax.experimental import pallas as pl
from jax.experimental.pallas import tpu as pltpu
from jax.sharding import PartitionSpec as P

F32 = jnp.float32
BF16 = jnp.bfloat16
MESH = pl.DeviceIdType.MESH
LOG2E = 1.4426950408889634
LN2 = 0.6931471805599453

ROWS = 128
CH = 4096
NS = 16
PLANES = 4
RING = 16
ZN = 8
HD = 128
GROUP = 4
STEPS = 16
HUGE = 3e38
MASKED = -1e30
RING_EVERY = 2
RING_START = 2
STORES = 4
OWN = CH // RING
SCALE = LOG2E / HD**0.5
ROW_CONTRACT = (((0,), (0,)), ((), ()))
LANE_CONTRACT = (((1,), (1,)), ((), ()))


def iota(shape, dim):
    return lax.broadcasted_iota(jnp.int32, shape, dim)


def tree_sum(terms):
    while len(terms) > 1:
        terms = [a + b for a, b in zip(terms[::2], terms[1::2])]
    return terms[0]


def silu(v):
    return (0.5 * v) * (1.0 + jnp.tanh(0.5 * v))


def kernel(
    x_hbm, gate_hbm, step_hbm, decay_ref, in_ref, out_map_ref, taps_ref, bias_ref, skip_ref, seg_ref,
    q_hbm, k_hbm, v_hbm,
    mixed_hbm, attended_hbm,
    xv, gv, sv, halo, u_ref, s_ref, cum_ref, gs_ref, y_ref, ends_ref, rates_ref, rates_t, bb_ref, cc_ref,
    masks_ref, bias_row, kv, docs, q_in, q_aug, o_buf, m_out, lengths, plane_len, totals, plane_in, plane_total, across_in, spread, entering,
    own_prefix,
    load_sem, halo_sem, qkv_send, qkv_recv, fwd_send, fwd_recv, bwd_send, bwd_recv, sib_send, sib_recv,
    len_send, len_recv, tot_send, tot_recv, acr_send, acr_recv, spr_send, spr_recv, o_send, o_recv, own_sem, store_sem,
):
    dp = lax.axis_index("dp")
    me = lax.axis_index("ctx")
    plane = me // RING
    r = me % RING
    z = r // 2
    core = r % 2

    def at(p, rr):
        return (dp, p * RING + rr)

    def remote(src, dst, send, recv, target):
        return pltpu.make_async_remote_copy(
            src_ref=src, dst_ref=dst, send_sem=send, recv_sem=recv, device_id=target, device_id_type=MESH
        )

    loads = [
        pltpu.make_async_copy(x_hbm, xv, load_sem.at[0]),
        pltpu.make_async_copy(step_hbm, sv, load_sem.at[1]),
        pltpu.make_async_copy(gate_hbm, gv, load_sem.at[2]),
    ]
    for load in loads:
        load.start()

    barrier = pltpu.get_barrier_semaphore()

    @pl.loop(1, RING)
    def _(j):
        pl.semaphore_signal(barrier, inc=1, device_id=at(plane, (r + j) % RING), device_id_type=MESH)

    @pl.loop(1, PLANES)
    def _(j):
        pl.semaphore_signal(barrier, inc=1, device_id=at((plane + j) % PLANES, r), device_id_type=MESH)

    count = PLANES * RING
    pl.semaphore_signal(barrier, inc=1, device_id=(dp, (me + 1) % count), device_id_type=MESH)
    pl.semaphore_signal(barrier, inc=1, device_id=(dp, (me + count - 1) % count), device_id_type=MESH)
    unit = (iota((16, HD), 0) == iota((16, HD), 1)).astype(BF16)
    doc_ids = iota((16, ROWS), 0).astype(F32)

    @pl.loop(0, PLANES * RING // 8, unroll=True)
    def _(g):
        rows = seg_ref[pl.ds(pl.multiple_of(g * 8, 8), 8), :].astype(F32)
        for i in range(8):
            hot = (doc_ids == rows[i : i + 1]).astype(BF16)
            cols = lax.dot_general(hot, unit, ROW_CONTRACT, preferred_element_type=F32)
            docs[g // 2, (g % 2) * 8 + i] = cols.astype(BF16)

    pl.semaphore_wait(barrier, RING - 1 + PLANES - 1 + 2)

    halo_copy = remote(
        x_hbm.at[pl.ds(ROWS - 16, 16), :], halo, halo_sem.at[0], halo_sem.at[1], (dp, (me + 1) % count)
    )
    halo_copy.start()

    def qkv_parts(p):
        return [
            (k_hbm.at[:, pl.ds(pl.multiple_of(p * HD, HD), HD)], kv.at[r, plane, :, pl.ds(0, HD)]),
            (v_hbm.at[:, pl.ds(pl.multiple_of(p * HD, HD), HD)], kv.at[r, plane, :, pl.ds(HD, HD)]),
            (q_hbm.at[:, pl.ds(pl.multiple_of(p * GROUP * HD, HD), GROUP * HD)], q_in.at[plane]),
        ]

    def qkv_copies(o, parts=(0, 1, 2)):
        p = (plane + o) % PLANES
        pairs = qkv_parts(p)
        return [
            remote(pairs[i][0], pairs[i][1], qkv_send.at[o, i], qkv_recv.at[o, i], at(p, r)) for i in parts
        ]

    for o in range(1, PLANES):
        for copy in qkv_copies(o, (0, 1)):
            copy.start()
    own_qkv = [pltpu.make_async_copy(s, d, own_sem.at[i]) for i, (s, d) in enumerate(qkv_parts(plane))]
    for copy in own_qkv:
        copy.start()

    p_ids, t_ids = iota((ROWS, ROWS), 0), iota((ROWS, ROWS), 1)
    perm = (t_ids == (p_ids % 8) * STEPS + p_ids // 8).astype(F32)
    perm_b = perm.astype(BF16)
    ones = jnp.ones((ROWS, ROWS), BF16)

    seg = seg_ref[...].astype(F32)
    block_ids = iota((PLANES * RING, ROWS), 0)

    def seg_row(b):
        return jnp.sum(jnp.where(block_ids == b, seg, 0.0), axis=0, keepdims=True)

    here = jnp.broadcast_to(seg_row(me), (8, ROWS))
    before = jnp.broadcast_to(jnp.where(me > 0, seg_row(me - 1), -1.0), (8, ROWS))
    lane8 = iota((8, ROWS), 1)
    for d in range(1, 4):
        ids = jnp.where(lane8 >= d, pltpu.roll(here, d, 1), pltpu.roll(before, d, 1))
        same = (ids == here).astype(F32)
        masks_ref[d] = jnp.dot((perm * same[0:1]).astype(BF16), ones, preferred_element_type=F32)
        if d == 1:
            fresh = ((ids != here) & (ids >= 0.0)).astype(F32)
            masks_ref[0] = jnp.dot((perm * fresh[0:1]).astype(BF16), ones, preferred_element_type=F32)

    repeat = (iota((NS, NS * 128), 0) == iota((NS, NS * 128), 1) // 128).astype(BF16)
    for src, dst in ((in_ref, bb_ref), (out_map_ref, cc_ref)):
        ordered = lax.dot_general(src[...], perm_b, LANE_CONTRACT, preferred_element_type=F32).astype(BF16)
        dst[...] = lax.dot_general(ordered, repeat, ROW_CONTRACT, preferred_element_type=F32)

    bias = bias_ref[...].astype(F32)
    for i in range(CH // 128):
        bias_row[:, pl.ds(i * 128, 128)] = bias[i : i + 1]

    @pl.loop(0, CH // 128)
    def _(cb):
        lanes = pl.ds(pl.multiple_of(cb * 128, 128), 128)
        rates = jnp.minimum(decay_ref[:, lanes], -1e-30) * LOG2E
        rates_t[:, lanes] = rates
        for n in range(NS):
            rates_ref[n, :, lanes] = jnp.broadcast_to(rates[n : n + 1], (8, 128))

    for p in range(PLANES):
        ids = seg_row(p * RING + r)
        cold = jnp.where((doc_ids != ids) & (doc_ids < 4.0), MASKED, 0.0).astype(BF16)
        cols = lax.dot_general(cold, unit, ROW_CONTRACT, preferred_element_type=F32).astype(BF16)
        for h in range(GROUP):
            q_aug[p, pl.ds(h * ROWS, ROWS), pl.ds(0, HD)] = cols

    def own_lanes(rr):
        return pl.ds(pl.multiple_of(rr * OWN, OWN), OWN)

    def lengths_copy(j):
        rr = (r + j) % RING
        return remote(lengths.at[:, own_lanes(rr)], plane_len.at[r], len_send.at[j], len_recv.at[j], at(plane, rr))

    def piece(rr, c):
        return kv.at[rr, c]

    def fwd(s, c):
        ref = piece(2 * ((z + ZN - s + 1) % ZN) + core, c)
        return remote(ref, ref, fwd_send.at[s, c], fwd_recv.at[s, c], at(plane, 2 * ((z + 1) % ZN) + core))

    def bwd(s, c):
        ref = piece(2 * ((z + s - 1) % ZN) + core, c)
        return remote(ref, ref, bwd_send.at[s, c], bwd_recv.at[s, c], at(plane, 2 * ((z + ZN - 1) % ZN) + core))

    def sibling(s, c):
        ref = piece(2 * ((z + ZN - s) % ZN) + core, c)
        return remote(ref, ref, sib_send.at[s, c], sib_recv.at[s, c], at(plane, 2 * z + 1 - core))

    def ring(s, c):
        return ([fwd(s, c)] if s < 4 or c < 2 else []) + ([bwd(s, c)] if s < 4 or c >= 2 else [])

    def ring_first():
        for copy in own_qkv[:2]:
            copy.wait()
        for o in range(1, PLANES):
            for copy in qkv_copies(o, (0, 1)):
                copy.wait_recv()
        for c in range(PLANES):
            for copy in ring(1, c):
                copy.start()
        for c in range(PLANES):
            sibling(0, c).start()

    def ring_next(s, c):
        for copy in ring(s, c):
            copy.wait_recv()
        sibling(s, c).start()

    def ring_turn(k):
        s, c = 1 + k // PLANES, k % PLANES
        fwd(s, c).wait_recv()
        bwd(s, c).wait_recv()

        @pl.when((s < 3) | (c < 2))
        def _():
            fwd(s + 1, c).start()

        @pl.when((s < 3) | (c >= 2))
        def _():
            bwd(s + 1, c).start()

        sibling(s, c).start()
        sibling(ZN - s, c).start()

    def shared(c):
        for s in range(ZN):
            sibling(s, c).wait_recv()

    for load in loads:
        load.wait()
    W = 1024

    @pl.loop(0, CH // W)
    def _(b):
        lanes = pl.ds(pl.multiple_of(b * W, W), W)
        sp = jnp.dot(perm_b, sv[:, lanes], preferred_element_type=F32)
        gp = jnp.dot(perm_b, gv[:, lanes], preferred_element_type=F32)
        fresh = jnp.concatenate([masks_ref[0]] * (W // 128), axis=1)
        steps = jnp.where(fresh > 0.0, HUGE, sp)
        s_ref[:, lanes] = steps
        running = steps[0:8]
        cum_ref[pl.ds(0, 8), lanes] = running
        for i in range(1, STEPS):
            running = running + steps[i * 8 : i * 8 + 8]
            cum_ref[pl.ds(i * 8, 8), lanes] = running
        gs_ref[:, lanes] = silu(gp)
        for by in (1, 2, 4):
            running = running + jnp.where(iota((8, W), 0) >= by, pltpu.roll(running, by, 0), 0.0)
        lengths[:, lanes] = running[7:8]

    halo_copy.wait()

    @pl.loop(0, CH // W)
    def _(b):
        lanes = pl.ds(pl.multiple_of(b * W, W), W)
        xp = jnp.dot(perm_b, xv[:, lanes], preferred_element_type=F32)
        edge = halo[:, lanes].astype(F32)
        first = iota((8, W), 0) == 0
        lead = []
        for d in (3, 2, 1):
            rolled = pltpu.roll(xp[(STEPS - d) * 8 : (STEPS - d + 1) * 8], 1, 0)
            lead.append(jnp.where(first, edge[16 - d : 17 - d], rolled))
        extended = jnp.concatenate(lead + [xp], axis=0)
        taps = taps_ref[:, lanes].astype(F32)
        summed = bias_row[:, lanes] + taps[3:4] * xp
        for d in range(1, 4):
            allowed = jnp.concatenate([masks_ref[d]] * (W // 128), axis=1)
            earlier = extended[(3 - d) * 8 : (3 - d) * 8 + ROWS]
            summed = summed + taps[3 - d : 4 - d] * earlier * allowed
        u_ref[:, lanes] = silu(summed).astype(BF16).astype(F32)

    ring_first()
    for o in range(1, PLANES):
        for copy in qkv_copies(o, (2,)):
            copy.start()

    @pl.loop(1, RING)
    def _(j):
        lengths_copy(j).start()

    plane_len[r] = lengths[:, own_lanes(r)]

    sub = iota((8, 128), 0)

    def prefix_parts(lanes):
        total = cum_ref[pl.ds((STEPS - 1) * 8, 8), lanes]
        two = total + pltpu.roll(total, 1, 0)
        four = two + pltpu.roll(two, 2, 0)
        return total, two, four

    def scan(cb):
        lanes = pl.ds(pl.multiple_of(cb * 128, 128), 128)
        total, two, four = prefix_parts(lanes)
        spans = [
            (1, jnp.where(sub >= 1, total, HUGE)),
            (2, jnp.where(sub >= 2, two, HUGE)),
            (4, jnp.where(sub >= 4, four, HUGE)),
        ]
        rates = [rates_ref[n, :, lanes] for n in range(NS)]
        states = [jnp.zeros((8, 128), F32) for _ in range(NS)]
        for i in range(STEPS):
            rows = pl.ds(i * 8, 8)
            steps, drive = s_ref[rows, lanes], u_ref[rows, lanes]
            reads = []
            for n in range(NS):
                coef = pl.ds(n * 128, 128)
                exponent = steps * rates[n]
                factor = jnp.exp2(exponent)
                square = jnp.tanh(exponent * (-LN2)) * (1.0 + factor * factor)
                weight = square * lax.rsqrt(square)
                states[n] = factor * states[n] + weight * (drive * bb_ref[rows, coef])
                reads.append(cc_ref[rows, coef] * states[n])
            y_ref[rows, lanes] = tree_sum(reads)
        for n in range(NS):
            state = states[n]
            for by, span in spans:
                state = state + jnp.exp2(rates[n] * span) * pltpu.roll(state, by, 0)
            totals[pl.ds(n, 1), lanes] = state[7:8]
            ends_ref[n, :, lanes] = jnp.where(sub >= 1, pltpu.roll(state, 1, 0), 0.0)

    @pl.loop(0, CH // 128 // RING_EVERY)
    def _(group):
        @pl.when((group >= RING_START) & (group < RING_START + 3 * PLANES))
        def _():
            ring_turn(group - RING_START)

        pl.loop(group * RING_EVERY, (group + 1) * RING_EVERY)(scan)

    ring_next(4, 0)
    ring_next(4, 1)

    def totals_copy(j):
        rr = (r + j) % RING
        return remote(totals.at[:, own_lanes(rr)], plane_in.at[r], tot_send.at[j], tot_recv.at[j], at(plane, rr))

    @pl.loop(1, RING)
    def _(j):
        totals_copy(j).start()

    plane_in[r] = totals[:, own_lanes(r)]

    for copy in own_qkv[2:]:
        copy.wait()
    for o in range(1, PLANES):
        for copy in qkv_copies(o, (2,)):
            copy.wait_recv()
    for p in range(PLANES):
        for h in range(GROUP):
            q_aug[p, pl.ds(h * ROWS, ROWS), pl.ds(HD, HD)] = q_in[p, :, pl.ds(h * HD, HD)]
    shared(0)
    shared(1)

    CK = RING * ROWS

    def out_copy(p):
        return remote(
            o_buf.at[p],
            attended_hbm.at[:, pl.ds(pl.multiple_of(plane * GROUP * HD, HD), GROUP * HD)],
            o_send.at[p],
            o_recv.at[plane],
            at(p, r),
        )

    def own_out_copy(p):
        return pltpu.make_async_copy(
            o_buf.at[p],
            attended_hbm.at[:, pl.ds(pl.multiple_of(plane * GROUP * HD, HD), GROUP * HD)],
            own_sem.at[3],
        )

    def step_scores(p, c):
        keys = kv[:, c, :, pl.ds(0, HD)].reshape(CK, HD)
        keys = jnp.concatenate([docs[c].reshape(CK, HD), keys], axis=1)
        scores = lax.dot_general(keys, q_aug[p], LANE_CONTRACT, preferred_element_type=F32)
        if c == p:
            limit = iota((CK, GROUP * ROWS), 1) % ROWS + r * ROWS
            scores = jnp.where(iota((CK, GROUP * ROWS), 0) <= limit, scores, MASKED)
        return scores

    held = {}

    def step_rest(p, c, scores):
        values = kv[:, c, :, pl.ds(HD, HD)].reshape(CK, HD)
        top = jnp.max(scores, axis=0, keepdims=True) * SCALE
        if c > 0:
            old_top, old_acc, old_total = held[p]
            top = jnp.maximum(old_top, top)
        probs = jnp.exp2(scores * SCALE - top)
        total = jnp.sum(probs, axis=0, keepdims=True)
        acc = lax.dot_general(values, probs.astype(BF16), ROW_CONTRACT, preferred_element_type=F32)
        if c > 0:
            shrink = jnp.exp2(old_top - top)
            acc, total = old_acc * shrink + acc, old_total * shrink + total
        held[p] = top, acc, total
        if c < p:
            return
        result = acc / total
        for h in range(GROUP):
            o_buf[p, :, pl.ds(h * HD, HD)] = result[:, h * ROWS : (h + 1) * ROWS].T.astype(BF16)

        @pl.when(plane != p)
        def _():
            out_copy(p).start()

        @pl.when(plane == p)
        def _():
            own_out_copy(p).start()

    order = [(0, 0), (1, 0), (1, 1), (2, 0), (2, 1), (3, 0), (3, 1), (2, 2), (3, 2), (3, 3)]
    ahead = [step_scores(*order[0])]

    def attend(first, end):
        for k in range(first, end):
            scores = ahead.pop()
            if k + 1 < len(order):
                ahead.append(step_scores(*order[k + 1]))
            step_rest(*order[k], scores)

    attend(0, 3)
    ring_next(4, 2)
    ring_next(4, 3)
    attend(3, 4)

    @pl.loop(1, RING)
    def _(j):
        totals_copy(j).wait_recv()
        lengths_copy(j).wait_recv()

    own_rates = rates_t[:, own_lanes(r)]
    state = jnp.zeros((NS, OWN), F32)
    length = jnp.zeros((1, OWN), F32)
    for i in range(RING):
        own_prefix[i, pl.ds(0, NS), :] = state
        own_prefix[i, pl.ds(NS, 8), :] = jnp.broadcast_to(length, (8, OWN))
        step = plane_len[i]
        state = jnp.exp2(own_rates * step) * state + plane_in[i]
        length = length + step
    plane_total[pl.ds(0, NS), :] = state
    plane_total[pl.ds(NS, 8), :] = jnp.broadcast_to(length, (8, OWN))

    def across_copy(o):
        p = (plane + o) % PLANES
        return remote(plane_total, across_in.at[plane], acr_send.at[o], acr_recv.at[o], at(p, r))

    for o in range(1, PLANES):
        across_copy(o).start()
    across_in[plane] = plane_total[...]

    attend(4, 6)

    for o in range(1, PLANES):
        across_copy(o).wait_recv()
    state = jnp.zeros((NS, OWN), F32)
    for p in range(PLANES - 1):
        moved = jnp.exp2(own_rates * across_in[p, pl.ds(NS, 1), :]) * state + across_in[p, pl.ds(0, NS), :]
        state = jnp.where(p < plane, moved, state)
    for i in range(RING):
        moved = own_prefix[i, pl.ds(0, NS), :] + jnp.exp2(own_rates * own_prefix[i, pl.ds(NS, 1), :]) * state
        spread[i] = moved.astype(BF16)

    def spread_copy(j):
        rr = (r + j) % RING
        return remote(spread.at[rr], entering.at[:, own_lanes(r)], spr_send.at[j], spr_recv.at[j], at(plane, rr))

    @pl.loop(1, RING)
    def _(j):
        spread_copy(j).start()

    entering[:, own_lanes(r)] = spread[r]

    shared(2)
    shared(3)
    attend(6, 10)

    @pl.loop(1, RING)
    def _(j):
        spread_copy(j).wait_recv()

    def store(s):
        lanes = pl.ds(s * (CH // STORES), CH // STORES)
        return pltpu.make_async_copy(m_out.at[:, lanes], mixed_hbm.at[:, lanes], store_sem.at[s])

    def finish(cb):
        lanes = pl.ds(pl.multiple_of(cb * 128, 128), 128)
        total, _, _ = prefix_parts(lanes)
        summed = total
        for by in (1, 2, 4):
            summed = summed + jnp.where(sub >= by, pltpu.roll(summed, by, 0), 0.0)
        lead = jnp.where(sub >= 1, pltpu.roll(summed, 1, 0), 0.0)
        rates = [rates_ref[n, :, lanes] for n in range(NS)]
        arriving = entering[:, lanes].astype(F32)
        states = [jnp.exp2(rates[n] * lead) * arriving[n : n + 1] + ends_ref[n, :, lanes] for n in range(NS)]
        skip = skip_ref[:, lanes]
        for i in range(STEPS):
            rows = pl.ds(i * 8, 8)
            since = cum_ref[rows, lanes]
            reads = [
                cc_ref[rows, pl.ds(n * 128, 128)] * (jnp.exp2(since * rates[n]) * states[n]) for n in range(NS)
            ]
            readout = y_ref[rows, lanes] + tree_sum(reads)
            s_ref[rows, lanes] = (readout + skip * u_ref[rows, lanes]) * gs_ref[rows, lanes]

    back = (p_ids == (t_ids % 8) * STEPS + t_ids // 8).astype(BF16)
    for s in range(STORES):
        pl.loop(s * (CH // 128 // STORES), (s + 1) * (CH // 128 // STORES))(finish)
        lanes = pl.ds(s * (CH // STORES), CH // STORES)
        m_out[:, lanes] = jnp.dot(back, s_ref[:, lanes].astype(BF16), preferred_element_type=F32).astype(BF16)
        store(s).start()

    for o in range(1, PLANES):
        for copy in qkv_copies(o):
            copy.wait_send()
        across_copy(o).wait_send()
    for c in range(PLANES):
        for s in range(1, 5):
            for copy in ring(s, c):
                copy.wait_send()
        for s in range(ZN):
            sibling(s, c).wait_send()

    @pl.loop(1, RING)
    def _(j):
        totals_copy(j).wait_send()
        lengths_copy(j).wait_send()
        spread_copy(j).wait_send()

    for p in range(PLANES):
        @pl.when(plane != p)
        def _():
            out_copy(p).wait_send()
            pltpu.make_async_remote_copy(
                src_ref=o_buf.at[p],
                dst_ref=attended_hbm.at[:, pl.ds(p * GROUP * HD, GROUP * HD)],
                send_sem=o_send.at[p],
                recv_sem=o_recv.at[p],
                device_id=at(p, r),
                device_id_type=MESH,
            ).wait_recv()

        @pl.when(plane == p)
        def _():
            own_out_copy(p).wait()

    for s in range(STORES):
        store(s).wait()


def hand_over(mixed, attended, mixed_out, attended_out, mixed_buf, attended_buf, sem):
    inward, outward = [], []
    for src, buf, dst, pieces in ((mixed, mixed_buf, mixed_out, 4), (attended, attended_buf, attended_out, 2)):
        for i in range(pieces):
            lanes = pl.ds(i * 1024, 1024)
            inward.append(pltpu.make_async_copy(src.at[:, lanes], buf.at[:, lanes], sem.at[0, len(inward)]))
            outward.append(pltpu.make_async_copy(buf.at[:, lanes], dst.at[:, lanes], sem.at[1, len(outward)]))
    for copy in inward:
        copy.start()
    for arrival, copy in zip(inward, outward):
        arrival.wait()
        copy.start()
    for copy in outward:
        copy.wait()


def on_device(
    mamba_input, gate_branch, step_size, decay_rates, input_map, output_map, mixing_weight, mixing_bias,
    skip_gain, segments, query_rows, key_rows, value_rows,
):
    hbm = pl.BlockSpec(memory_space=pl.ANY)
    vmem = pl.BlockSpec(memory_space=pltpu.VMEM)
    big = pltpu.VMEM((ROWS, CH), F32)
    dma = pltpu.SemaphoreType.DMA
    mixed, attended = pl.pallas_call(
        kernel,
        out_shape=(
            jax.ShapeDtypeStruct((ROWS, CH), BF16),
            jax.ShapeDtypeStruct((ROWS, PLANES * GROUP * HD), BF16),
        ),
        in_specs=[hbm] * 3 + [vmem] * 7 + [hbm] * 3,
        out_specs=(hbm, hbm),
        scratch_shapes=[
            pltpu.VMEM((ROWS, CH), BF16),
            pltpu.VMEM((ROWS, CH), BF16),
            pltpu.VMEM((ROWS, CH), BF16),
            pltpu.VMEM((16, CH), BF16),
            big, big, big, big, big,
            pltpu.VMEM((NS, 8, CH), F32),
            pltpu.VMEM((NS, 8, CH), F32),
            pltpu.VMEM((NS, CH), F32),
            pltpu.VMEM((ROWS, NS * 128), F32),
            pltpu.VMEM((ROWS, NS * 128), F32),
            pltpu.VMEM((4, ROWS, ROWS), F32),
            pltpu.VMEM((1, CH), F32),
            pltpu.VMEM((RING, PLANES, ROWS, 2 * HD), BF16),
            pltpu.VMEM((PLANES, RING, ROWS, HD), BF16),
            pltpu.VMEM((PLANES, ROWS, GROUP * HD), BF16),
            pltpu.VMEM((PLANES, GROUP * ROWS, 2 * HD), BF16),
            pltpu.VMEM((PLANES, ROWS, GROUP * HD), BF16),
            pltpu.VMEM((ROWS, CH), BF16),
            pltpu.VMEM((1, CH), F32),
            pltpu.VMEM((RING, 1, OWN), F32),
            pltpu.VMEM((NS, CH), F32),
            pltpu.VMEM((RING, NS, OWN), F32),
            pltpu.VMEM((NS + 8, OWN), F32),
            pltpu.VMEM((PLANES, NS + 8, OWN), F32),
            pltpu.VMEM((RING, NS, OWN), BF16),
            pltpu.VMEM((NS, CH), BF16),
            pltpu.VMEM((RING, NS + 8, OWN), F32),
            dma((3,)), dma((2,)), dma((4, 3)), dma((4, 3)),
            dma((5, 4)), dma((5, 4)), dma((5, 4)), dma((5, 4)), dma((ZN, 4)), dma((ZN, 4)),
            dma((RING,)), dma((RING,)), dma((RING,)), dma((RING,)), dma((PLANES,)), dma((PLANES,)), dma((RING,)), dma((RING,)),
            dma((PLANES,)), dma((PLANES,)), dma((4,)), dma((STORES,)),
        ],
        compiler_params=pltpu.CompilerParams(
            collective_id=0, has_side_effects=True, vmem_limit_bytes=60 * 2**20
        ),
        name="mixer",
    )(
        mamba_input, gate_branch, step_size, decay_rates.T, input_map.T, output_map.T, mixing_weight,
        mixing_bias.reshape(CH // 128, 128), skip_gain.reshape(1, CH), segments.reshape(PLANES * RING, ROWS),
        query_rows, key_rows, value_rows,
    )
    shapes = (jax.ShapeDtypeStruct(mixed.shape, BF16), jax.ShapeDtypeStruct(attended.shape, BF16))
    return pl.pallas_call(
        hand_over,
        out_shape=shapes,
        in_specs=[hbm] * 2,
        out_specs=(hbm, hbm),
        scratch_shapes=[
            pltpu.VMEM(mixed.shape, BF16), pltpu.VMEM(attended.shape, BF16), dma((2, 6)),
        ],
        compiler_params=pltpu.CompilerParams(vmem_limit_bytes=60 * 2**20),
        name="hand_over",
    )(mixed, attended)


def solution(mesh):
    split = P(("dp", "ctx"), None)
    in_specs = (
        split, split, split, P("dp", None), split, split, P(), P(), P(), P("dp"), split, split, split,
    )
    return jax.shard_map(
        on_device, mesh=mesh, in_specs=in_specs, out_specs=(split, split), check_vma=False
    )
```

time: 95.9 us -> 73.8 us (0.77)
  Pallas kernels: 84.9 us -> 72 us
  local copies, waits for them, and re-layouts: 10.2 us -> 0 us
    pallas_call x1, Pallas kernels: 84.9 us -> 69.8 us  [on_device(): pl.pallas_call(kernel, out_shape=(jax.ShapeDtypeStruct((ROWS, CH), BF16),...]
    unnamed x7 -> x0, local copies, waits for them, and re-layouts: 8.85 us -> none
    pallas_call x0 -> x1, Pallas kernels: none -> 2.19 us  [on_device(): pl.pallas_call(hand_over, out_shape=shapes, in_specs=[hbm] * 2, out_specs...]
    reshape x1 -> x0, local copies, waits for them, and re-layouts: 1.31 us -> none  [on_device(): mixing_bias.reshape(1, CH)]
where the time goes in v2:
time: 73.8 us; the launch traced here: 72.8 us
  Pallas kernels  72 us (98%)
  between operations  0.8 us (1%)
    pallas_call x1, Pallas kernels, on_device(): pl.pallas_call(kernel, out_shape=(jax.ShapeDtypeStruct((ROWS, CH), BF16),...  69.8 us
    pallas_call x1, Pallas kernels, on_device(): pl.pallas_call(hand_over, out_shape=shapes, in_specs=[hbm] * 2, out_specs...  2.19 us

profile of v2, /device:TPU:1, one launch (start us, length us, event | category | flops | bytes accessed | tf_op | source)
XLA Modules:
  0.0 72.8 jit_solution(18168016595909064792)
XLA Ops:
  0.6 69.8 %mixer.1 = (bf16[128,4096]{1,0:T(8,128)(2,1)}, bf16[128,2048]{1,0:T(8,128)(2,1)}) custom-call(bf16[128,4096]{1,0:T(8,128)(2,1)} %x_hbm.1, bf16[128,4096]{1,0:T(8,128)(2,1)} %gate_hbm.1, bf16[128,4096]{1,0:T(8,128)(2,1)} %step_hbm.1, f32[16,4096]{1,0:T(8,128)} %bitcast.6, bf16[16,128]{1,0:T(8,128)(2,1)} %bitcast.10, bf16[16,128]{1,0:T(8,128)(2,1)} %bitcast.11, ...), custom_call_target="tpu_custom_call" | custom-call | tf_op jit(solution)/shard_map/mixer/pallas_call | solution.py:586
  70.4 2.2 %hand_over.1 = (bf16[128,4096]{1,0:T(8,128)(2,1)}, bf16[128,2048]{1,0:T(8,128)(2,1)}) custom-call(bf16[128,4096]{1,0:T(8,128)(2,1)} %get-tuple-element.4.mixed, bf16[128,2048]{1,0:T(8,128)(2,1)} %get-tuple-element.5.attended), custom_call_target="tpu_custom_call" | custom-call | tf_op jit(solution)/shard_map/hand_over/pallas_call | solution.py:637

commit v3 on v2

--- a/solution.py
+++ b/solution.py
@@ -24,8 +24,12 @@
 STEPS = 16
 HUGE = 3e38
 MASKED = -1e30
-RING_EVERY = 2
-RING_START = 2
+RING_EVERY = 1
+RING_TURNS = (
+    (3, 1, 0), (4, 1, 1), (6, 2, 0), (8, 2, 1), (9, 1, 2), (10, 3, 0), (11, 1, 3), (13, 2, 2), (14, 3, 1), (15, 2, 3)
+)
+RING_OWN = ((4, 2), (7, 3))
+RING_END = 14
 STORES = 4
 OWN = CH // RING
 SCALE = LOG2E / HD**0.5
@@ -52,7 +56,7 @@
     q_hbm, k_hbm, v_hbm,
     mixed_hbm, attended_hbm,
     xv, gv, sv, halo, u_ref, s_ref, cum_ref, gs_ref, y_ref, ends_ref, rates_ref, rates_t, bb_ref, cc_ref,
-    masks_ref, bias_row, kv, docs, q_in, q_aug, o_buf, m_out, lengths, plane_len, totals, plane_in, plane_total, across_in, spread, entering,
+    masks_ref, bias_row, kv, docs, q_in, q_aug, o_buf, m_out, lengths, plane_len, totals, plane_in, plane_total, across_in, entered, spread, entering,
     own_prefix,
     load_sem, halo_sem, qkv_send, qkv_recv, fwd_send, fwd_recv, bwd_send, bwd_recv, sib_send, sib_recv,
     len_send, len_recv, tot_send, tot_recv, acr_send, acr_recv, spr_send, spr_recv, o_send, o_recv, own_sem, store_sem,
@@ -203,25 +207,22 @@
     def ring(s, c):
         return ([fwd(s, c)] if s < 4 or c < 2 else []) + ([bwd(s, c)] if s < 4 or c >= 2 else [])
 
+    def own_piece(c):
+        for copy in ring(1, c):
+            copy.start()
+
     def ring_first():
         for copy in own_qkv[:2]:
             copy.wait()
         for o in range(1, PLANES):
             for copy in qkv_copies(o, (0, 1)):
                 copy.wait_recv()
-        for c in range(PLANES):
-            for copy in ring(1, c):
-                copy.start()
+        for c in (0, 1):
+            own_piece(c)
         for c in range(PLANES):
             sibling(0, c).start()
 
-    def ring_next(s, c):
-        for copy in ring(s, c):
-            copy.wait_recv()
-        sibling(s, c).start()
-
-    def ring_turn(k):
-        s, c = 1 + k // PLANES, k % PLANES
+    def ring_turn(s, c):
         fwd(s, c).wait_recv()
         bwd(s, c).wait_recv()
 
@@ -235,6 +236,11 @@
 
         sibling(s, c).start()
         sibling(ZN - s, c).start()
+
+    def ring_last(c):
+        for copy in ring(4, c):
+            copy.wait_recv()
+        sibling(4, c).start()
 
     def shared(c):
         for s in range(ZN):
@@ -302,46 +308,64 @@
         four = two + pltpu.roll(two, 2, 0)
         return total, two, four
 
-    def scan(cb):
-        lanes = pl.ds(pl.multiple_of(cb * 128, 128), 128)
-        total, two, four = prefix_parts(lanes)
-        spans = [
-            (1, jnp.where(sub >= 1, total, HUGE)),
-            (2, jnp.where(sub >= 2, two, HUGE)),
-            (4, jnp.where(sub >= 4, four, HUGE)),
-        ]
-        rates = [rates_ref[n, :, lanes] for n in range(NS)]
-        states = [jnp.zeros((8, 128), F32) for _ in range(NS)]
-        for i in range(STEPS):
-            rows = pl.ds(i * 8, 8)
-            steps, drive = s_ref[rows, lanes], u_ref[rows, lanes]
-            reads = []
-            for n in range(NS):
-                coef = pl.ds(n * 128, 128)
-                exponent = steps * rates[n]
-                factor = jnp.exp2(exponent)
-                square = jnp.tanh(exponent * (-LN2)) * (1.0 + factor * factor)
-                weight = square * lax.rsqrt(square)
-                states[n] = factor * states[n] + weight * (drive * bb_ref[rows, coef])
-                reads.append(cc_ref[rows, coef] * states[n])
-            y_ref[rows, lanes] = tree_sum(reads)
-        for n in range(NS):
-            state = states[n]
-            for by, span in spans:
-                state = state + jnp.exp2(rates[n] * span) * pltpu.roll(state, by, 0)
-            totals[pl.ds(n, 1), lanes] = state[7:8]
-            ends_ref[n, :, lanes] = jnp.where(sub >= 1, pltpu.roll(state, 1, 0), 0.0)
-
-    @pl.loop(0, CH // 128 // RING_EVERY)
+    def scan(pair):
+        blocks = [pl.ds(pl.multiple_of(pair * 256 + b * 128, 128), 128) for b in range(2)]
+        spans = []
+        for lanes in blocks:
+            total, two, four = prefix_parts(lanes)
+            spans.append([
+                (1, jnp.where(sub >= 1, total, HUGE)),
+                (2, jnp.where(sub >= 2, two, HUGE)),
+                (4, jnp.where(sub >= 4, four, HUGE)),
+            ])
+        for first in range(0, NS, NS // 2):
+            held_states = range(first, first + NS // 2)
+            rates = [[rates_ref[n, :, lanes] for n in held_states] for lanes in blocks]
+            states = [[jnp.zeros((8, 128), F32) for n in held_states] for lanes in blocks]
+            for i in range(STEPS):
+                rows = pl.ds(i * 8, 8)
+                steps = [s_ref[rows, lanes] for lanes in blocks]
+                drives = [u_ref[rows, lanes] for lanes in blocks]
+                reads = [[], []]
+                for k, n in enumerate(held_states):
+                    into = bb_ref[rows, pl.ds(n * 128, 128)]
+                    out_of = cc_ref[rows, pl.ds(n * 128, 128)]
+                    for b in range(2):
+                        exponent = steps[b] * rates[b][k]
+                        factor = jnp.exp2(exponent)
+                        ratio = jnp.tanh(exponent * (-0.5 * LN2))
+                        part = ratio * lax.rsqrt(ratio) * (drives[b] * into)
+                        states[b][k] = factor * (states[b][k] + part) + part
+                        reads[b].append(out_of * states[b][k])
+                for b, lanes in enumerate(blocks):
+                    readout = tree_sum(reads[b])
+                    y_ref[rows, lanes] = readout if first == 0 else y_ref[rows, lanes] + readout
+            for b, lanes in enumerate(blocks):
+                for k, n in enumerate(held_states):
+                    state = states[b][k]
+                    for by, span in spans[b]:
+                        state = state + jnp.exp2(rates[b][k] * span) * pltpu.roll(state, by, 0)
+                    totals[pl.ds(n, 1), lanes] = state[7:8]
+                    ends_ref[n, :, lanes] = jnp.where(sub >= 1, pltpu.roll(state, 1, 0), 0.0)
+
+    @pl.loop(0, CH // 256 // RING_EVERY)
     def _(group):
-        @pl.when((group >= RING_START) & (group < RING_START + 3 * PLANES))
-        def _():
-            ring_turn(group - RING_START)
+        code = sum(jnp.where(group == look, s * PLANES + c, 0) for look, s, c in RING_TURNS)
+
+        @pl.when(code > 0)
+        def _():
+            ring_turn(code // PLANES, code % PLANES)
+
+        for look, c in RING_OWN:
+            @pl.when(group == look)
+            def _():
+                own_piece(c)
+
+        @pl.when(group == RING_END)
+        def _():
+            ring_last(0)
 
         pl.loop(group * RING_EVERY, (group + 1) * RING_EVERY)(scan)
-
-    ring_next(4, 0)
-    ring_next(4, 1)
 
     def totals_copy(j):
         rr = (r + j) % RING
@@ -362,7 +386,6 @@
         for h in range(GROUP):
             q_aug[p, pl.ds(h * ROWS, ROWS), pl.ds(HD, HD)] = q_in[p, :, pl.ds(h * HD, HD)]
     shared(0)
-    shared(1)
 
     CK = RING * ROWS
 
@@ -420,7 +443,7 @@
         def _():
             own_out_copy(p).start()
 
-    order = [(0, 0), (1, 0), (1, 1), (2, 0), (2, 1), (3, 0), (3, 1), (2, 2), (3, 2), (3, 3)]
+    order = [(0, 0), (1, 0), (2, 0), (3, 0), (1, 1), (2, 1), (3, 1), (2, 2), (3, 2), (3, 3)]
     ahead = [step_scores(*order[0])]
 
     def attend(first, end):
@@ -430,10 +453,12 @@
                 ahead.append(step_scores(*order[k + 1]))
             step_rest(*order[k], scores)
 
-    attend(0, 3)
-    ring_next(4, 2)
-    ring_next(4, 3)
-    attend(3, 4)
+    attend(0, 1)
+    ring_turn(3, 2)
+    attend(1, 2)
+    ring_last(1)
+    ring_turn(3, 3)
+    attend(2, 3)
 
     @pl.loop(1, RING)
     def _(j):
@@ -458,16 +483,28 @@
 
     for o in range(1, PLANES):
         across_copy(o).start()
-    across_in[plane] = plane_total[...]
-
-    attend(4, 6)
+
+    shared(1)
+    attend(3, 4)
+    ring_last(2)
+    attend(4, 5)
+    ring_last(3)
+    attend(5, 6)
+    shared(2)
 
     for o in range(1, PLANES):
-        across_copy(o).wait_recv()
-    state = jnp.zeros((NS, OWN), F32)
+        @pl.when(o <= plane)
+        def _():
+            across_copy(o).wait_recv()
+
+    entered[...] = jnp.zeros((NS, OWN), F32)
     for p in range(PLANES - 1):
-        moved = jnp.exp2(own_rates * across_in[p, pl.ds(NS, 1), :]) * state + across_in[p, pl.ds(0, NS), :]
-        state = jnp.where(p < plane, moved, state)
+        @pl.when(p < plane)
+        def _():
+            moved = jnp.exp2(own_rates * across_in[p, pl.ds(NS, 1), :]) * entered[...]
+            entered[...] = moved + across_in[p, pl.ds(0, NS), :]
+
+    state = entered[...]
     for i in range(RING):
         moved = own_prefix[i, pl.ds(0, NS), :] + jnp.exp2(own_rates * own_prefix[i, pl.ds(NS, 1), :]) * state
         spread[i] = moved.astype(BF16)
@@ -482,9 +519,9 @@
 
     entering[:, own_lanes(r)] = spread[r]
 
-    shared(2)
+    attend(6, 8)
     shared(3)
-    attend(6, 10)
+    attend(8, 10)
 
     @pl.loop(1, RING)
     def _(j):
@@ -525,6 +562,11 @@
         for copy in qkv_copies(o):
             copy.wait_send()
         across_copy(o).wait_send()
+
+        @pl.when(o > plane)
+        def _():
+            across_copy(o).wait_recv()
+
     for c in range(PLANES):
         for s in range(1, 5):
             for copy in ring(s, c):
@@ -616,6 +658,7 @@
             pltpu.VMEM((RING, NS, OWN), F32),
             pltpu.VMEM((NS + 8, OWN), F32),
             pltpu.VMEM((PLANES, NS + 8, OWN), F32),
+            pltpu.VMEM((NS, OWN), F32),
             pltpu.VMEM((RING, NS, OWN), BF16),
             pltpu.VMEM((NS, CH), BF16),
             pltpu.VMEM((RING, NS + 8, OWN), F32),

time: 73.8 us -> 71.4 us (0.967); the launches traced: 72.8 us -> 71.2 us
  Pallas kernels: 72 us -> 70.4 us
    pallas_call x1, Pallas kernels: 69.8 us -> 68.2 us  [on_device(): pl.pallas_call(kernel, out_shape=(jax.ShapeDtypeStruct((ROWS, CH), BF16),...]
where the time goes in v3:
time: 71.4 us; the launch traced here: 71.2 us
  Pallas kernels  70.4 us (99%)
  between operations  0.8 us (1%)
    pallas_call x1, Pallas kernels, on_device(): pl.pallas_call(kernel, out_shape=(jax.ShapeDtypeStruct((ROWS, CH), BF16),...  68.2 us
    pallas_call x1, Pallas kernels, on_device(): pl.pallas_call(hand_over, out_shape=shapes, in_specs=[hbm] * 2, out_specs...  2.19 us

profile of v3, /device:TPU:1, one launch (start us, length us, event | category | flops | bytes accessed | tf_op | source)
XLA Modules:
  0.0 71.2 jit_solution(12859789467216554497)
XLA Ops:
  0.6 68.2 %mixer.1 = (bf16[128,4096]{1,0:T(8,128)(2,1)}, bf16[128,2048]{1,0:T(8,128)(2,1)}) custom-call(bf16[128,4096]{1,0:T(8,128)(2,1)} %x_hbm.1, bf16[128,4096]{1,0:T(8,128)(2,1)} %gate_hbm.1, bf16[128,4096]{1,0:T(8,128)(2,1)} %step_hbm.1, f32[16,4096]{1,0:T(8,128)} %bitcast.6, bf16[16,128]{1,0:T(8,128)(2,1)} %bitcast.10, bf16[16,128]{1,0:T(8,128)(2,1)} %bitcast.11, ...), custom_call_target="tpu_custom_call" | custom-call | tf_op jit(solution)/shard_map/mixer/pallas_call | solution.py:628
  68.9 2.2 %hand_over.1 = (bf16[128,4096]{1,0:T(8,128)(2,1)}, bf16[128,2048]{1,0:T(8,128)(2,1)}) custom-call(bf16[128,4096]{1,0:T(8,128)(2,1)} %get-tuple-element.4.mixed, bf16[128,2048]{1,0:T(8,128)(2,1)} %get-tuple-element.5.attended), custom_call_target="tpu_custom_call" | custom-call | tf_op jit(solution)/shard_map/hand_over/pallas_call | solution.py:680

commit v4 on v3

--- a/solution.py
+++ b/solution.py
@@ -55,7 +55,7 @@
     x_hbm, gate_hbm, step_hbm, decay_ref, in_ref, out_map_ref, taps_ref, bias_ref, skip_ref, seg_ref,
     q_hbm, k_hbm, v_hbm,
     mixed_hbm, attended_hbm,
-    xv, gv, sv, halo, u_ref, s_ref, cum_ref, gs_ref, y_ref, ends_ref, rates_ref, rates_t, bb_ref, cc_ref,
+    xv, gv, sv, halo, u_ref, s_ref, cum_ref, gs_ref, y_ref, ends_ref, rates_t, bb_ref, cc_ref,
     masks_ref, bias_row, kv, docs, q_in, q_aug, o_buf, m_out, lengths, plane_len, totals, plane_in, plane_total, across_in, entered, spread, entering,
     own_prefix,
     load_sem, halo_sem, qkv_send, qkv_recv, fwd_send, fwd_recv, bwd_send, bwd_recv, sib_send, sib_recv,
@@ -167,13 +167,10 @@
     for i in range(CH // 128):
         bias_row[:, pl.ds(i * 128, 128)] = bias[i : i + 1]
 
-    @pl.loop(0, CH // 128)
-    def _(cb):
-        lanes = pl.ds(pl.multiple_of(cb * 128, 128), 128)
-        rates = jnp.minimum(decay_ref[:, lanes], -1e-30) * LOG2E
-        rates_t[:, lanes] = rates
-        for n in range(NS):
-            rates_ref[n, :, lanes] = jnp.broadcast_to(rates[n : n + 1], (8, 128))
+    rates_t[...] = jnp.minimum(decay_ref[...], -1e-30) * LOG2E
+
+    def rate_rows(n, lanes):
+        return jnp.broadcast_to(rates_t[pl.ds(n, 1), lanes], (8, 128))
 
     for p in range(PLANES):
         ids = seg_row(p * RING + r)
@@ -248,7 +245,7 @@
 
     for load in loads:
         load.wait()
-    W = 1024
+    W = 2048
 
     @pl.loop(0, CH // W)
     def _(b):
@@ -320,7 +317,7 @@
             ])
         for first in range(0, NS, NS // 2):
             held_states = range(first, first + NS // 2)
-            rates = [[rates_ref[n, :, lanes] for n in held_states] for lanes in blocks]
+            rates = [[rate_rows(n, lanes) for n in held_states] for lanes in blocks]
             states = [[jnp.zeros((8, 128), F32) for n in held_states] for lanes in blocks]
             for i in range(STEPS):
                 rows = pl.ds(i * 8, 8)
@@ -531,29 +528,44 @@
         lanes = pl.ds(s * (CH // STORES), CH // STORES)
         return pltpu.make_async_copy(m_out.at[:, lanes], mixed_hbm.at[:, lanes], store_sem.at[s])
 
-    def finish(cb):
-        lanes = pl.ds(pl.multiple_of(cb * 128, 128), 128)
-        total, _, _ = prefix_parts(lanes)
-        summed = total
-        for by in (1, 2, 4):
-            summed = summed + jnp.where(sub >= by, pltpu.roll(summed, by, 0), 0.0)
-        lead = jnp.where(sub >= 1, pltpu.roll(summed, 1, 0), 0.0)
-        rates = [rates_ref[n, :, lanes] for n in range(NS)]
-        arriving = entering[:, lanes].astype(F32)
-        states = [jnp.exp2(rates[n] * lead) * arriving[n : n + 1] + ends_ref[n, :, lanes] for n in range(NS)]
-        skip = skip_ref[:, lanes]
-        for i in range(STEPS):
-            rows = pl.ds(i * 8, 8)
-            since = cum_ref[rows, lanes]
-            reads = [
-                cc_ref[rows, pl.ds(n * 128, 128)] * (jnp.exp2(since * rates[n]) * states[n]) for n in range(NS)
+    def finish(pair):
+        blocks = [pl.ds(pl.multiple_of(pair * 256 + b * 128, 128), 128) for b in range(2)]
+        leads, arriving = [], []
+        for lanes in blocks:
+            summed, _, _ = prefix_parts(lanes)
+            for by in (1, 2, 4):
+                summed = summed + jnp.where(sub >= by, pltpu.roll(summed, by, 0), 0.0)
+            leads.append(jnp.where(sub >= 1, pltpu.roll(summed, 1, 0), 0.0))
+            arriving.append(entering[:, lanes].astype(F32))
+        for first in range(0, NS, NS // 2):
+            held_states = range(first, first + NS // 2)
+            rates = [[rate_rows(n, lanes) for n in held_states] for lanes in blocks]
+            states = [
+                [
+                    jnp.exp2(rates[b][k] * leads[b]) * arriving[b][n : n + 1] + ends_ref[n, :, lanes]
+                    for k, n in enumerate(held_states)
+                ]
+                for b, lanes in enumerate(blocks)
             ]
-            readout = y_ref[rows, lanes] + tree_sum(reads)
-            s_ref[rows, lanes] = (readout + skip * u_ref[rows, lanes]) * gs_ref[rows, lanes]
+            for i in range(STEPS):
+                rows = pl.ds(i * 8, 8)
+                since = [cum_ref[rows, lanes] for lanes in blocks]
+                reads = [[], []]
+                for k, n in enumerate(held_states):
+                    out_of = cc_ref[rows, pl.ds(n * 128, 128)]
+                    for b in range(2):
+                        reads[b].append(out_of * (jnp.exp2(since[b] * rates[b][k]) * states[b][k]))
+                for b, lanes in enumerate(blocks):
+                    readout = y_ref[rows, lanes] + tree_sum(reads[b])
+                    if first == 0:
+                        y_ref[rows, lanes] = readout
+                    else:
+                        direct = skip_ref[:, lanes] * u_ref[rows, lanes]
+                        s_ref[rows, lanes] = (readout + direct) * gs_ref[rows, lanes]
 
     back = (p_ids == (t_ids % 8) * STEPS + t_ids // 8).astype(BF16)
     for s in range(STORES):
-        pl.loop(s * (CH // 128 // STORES), (s + 1) * (CH // 128 // STORES))(finish)
+        pl.loop(s * (CH // 256 // STORES), (s + 1) * (CH // 256 // STORES))(finish)
         lanes = pl.ds(s * (CH // STORES), CH // STORES)
         m_out[:, lanes] = jnp.dot(back, s_ref[:, lanes].astype(BF16), preferred_element_type=F32).astype(BF16)
         store(s).start()
@@ -639,7 +651,6 @@
             pltpu.VMEM((ROWS, CH), BF16),
             pltpu.VMEM((16, CH), BF16),
             big, big, big, big, big,
-            pltpu.VMEM((NS, 8, CH), F32),
             pltpu.VMEM((NS, 8, CH), F32),
             pltpu.VMEM((NS, CH), F32),
             pltpu.VMEM((ROWS, NS * 128), F32),

time: 71.4 us -> 71 us (level)
  no operation moved by 1% of the time
where the time goes in v4:
time: 71 us; the launch traced here: 70.8 us
  Pallas kernels  70 us (99%)
  between operations  0.8 us (1%)
    pallas_call x1, Pallas kernels, on_device(): pl.pallas_call(kernel, out_shape=(jax.ShapeDtypeStruct((ROWS, CH), BF16),...  67.8 us
    pallas_call x1, Pallas kernels, on_device(): pl.pallas_call(hand_over, out_shape=shapes, in_specs=[hbm] * 2, out_specs...  2.19 us

profile of v4, /device:TPU:1, one launch (start us, length us, event | category | flops | bytes accessed | tf_op | source)
XLA Modules:
  0.0 70.8 jit_solution(679988218160273706)
XLA Ops:
  0.6 67.8 %mixer.1 = (bf16[128,4096]{1,0:T(8,128)(2,1)}, bf16[128,2048]{1,0:T(8,128)(2,1)}) custom-call(bf16[128,4096]{1,0:T(8,128)(2,1)} %x_hbm.1, bf16[128,4096]{1,0:T(8,128)(2,1)} %gate_hbm.1, bf16[128,4096]{1,0:T(8,128)(2,1)} %step_hbm.1, f32[16,4096]{1,0:T(8,128)} %bitcast.6, bf16[16,128]{1,0:T(8,128)(2,1)} %bitcast.10, bf16[16,128]{1,0:T(8,128)(2,1)} %bitcast.11, ...), custom_call_target="tpu_custom_call" | custom-call | tf_op jit(solution)/shard_map/mixer/pallas_call | solution.py:640
  68.5 2.2 %hand_over.1 = (bf16[128,4096]{1,0:T(8,128)(2,1)}, bf16[128,2048]{1,0:T(8,128)(2,1)}) custom-call(bf16[128,4096]{1,0:T(8,128)(2,1)} %get-tuple-element.4.mixed, bf16[128,2048]{1,0:T(8,128)(2,1)} %get-tuple-element.5.attended), custom_call_target="tpu_custom_call" | custom-call | tf_op jit(solution)/shard_map/hand_over/pallas_call | solution.py:691

commit v5 on v4

--- a/solution.py
+++ b/solution.py
@@ -30,6 +30,7 @@
 )
 RING_OWN = ((4, 2), (7, 3))
 RING_END = 14
+RING_REST = 5
 STORES = 4
 OWN = CH // RING
 SCALE = LOG2E / HD**0.5
@@ -216,8 +217,7 @@
                 copy.wait_recv()
         for c in (0, 1):
             own_piece(c)
-        for c in range(PLANES):
-            sibling(0, c).start()
+        sibling(0, 0).start()
 
     def ring_turn(s, c):
         fwd(s, c).wait_recv()
@@ -287,10 +287,6 @@
         u_ref[:, lanes] = silu(summed).astype(BF16).astype(F32)
 
     ring_first()
-    for o in range(1, PLANES):
-        for copy in qkv_copies(o, (2,)):
-            copy.start()
-
     @pl.loop(1, RING)
     def _(j):
         lengths_copy(j).start()
@@ -357,6 +353,14 @@
             @pl.when(group == look)
             def _():
                 own_piece(c)
+
+        @pl.when(group == RING_REST)
+        def _():
+            for c in range(1, PLANES):
+                sibling(0, c).start()
+            for o in range(1, PLANES):
+                for copy in qkv_copies(o, (2,)):
+                    copy.start()
 
         @pl.when(group == RING_END)
         def _():

time: 71 us -> 70.9 us (level)
  no operation moved by 1% of the time
where the time goes in v5:
time: 70.9 us; the launch traced here: 70.8 us
  Pallas kernels  70 us (99%)
  between operations  0.8 us (1%)
    pallas_call x1, Pallas kernels, on_device(): pl.pallas_call(kernel, out_shape=(jax.ShapeDtypeStruct((ROWS, CH), BF16),...  67.8 us
    pallas_call x1, Pallas kernels, on_device(): pl.pallas_call(hand_over, out_shape=shapes, in_specs=[hbm] * 2, out_specs...  2.19 us

profile of v5, /device:TPU:1, one launch (start us, length us, event | category | flops | bytes accessed | tf_op | source)
XLA Modules:
  0.0 70.8 jit_solution(1575412862386731812)
XLA Ops:
  0.6 67.8 %mixer.1 = (bf16[128,4096]{1,0:T(8,128)(2,1)}, bf16[128,2048]{1,0:T(8,128)(2,1)}) custom-call(bf16[128,4096]{1,0:T(8,128)(2,1)} %x_hbm.1, bf16[128,4096]{1,0:T(8,128)(2,1)} %gate_hbm.1, bf16[128,4096]{1,0:T(8,128)(2,1)} %step_hbm.1, f32[16,4096]{1,0:T(8,128)} %bitcast.6, bf16[16,128]{1,0:T(8,128)(2,1)} %bitcast.10, bf16[16,128]{1,0:T(8,128)(2,1)} %bitcast.11, ...), custom_call_target="tpu_custom_call" | custom-call | tf_op jit(solution)/shard_map/mixer/pallas_call | solution.py:644
  68.4 2.2 %hand_over.1 = (bf16[128,4096]{1,0:T(8,128)(2,1)}, bf16[128,2048]{1,0:T(8,128)(2,1)}) custom-call(bf16[128,4096]{1,0:T(8,128)(2,1)} %get-tuple-element.4.mixed, bf16[128,2048]{1,0:T(8,128)(2,1)} %get-tuple-element.5.attended), custom_call_target="tpu_custom_call" | custom-call | tf_op jit(solution)/shard_map/hand_over/pallas_call | solution.py:695
